TPU v7x, 512 devices: a whole 4x8x8 slice. The times are simulated.
512 devices in a mesh: dp: 2 (over core), seq: 32 (over x, y), tensor: 8 (over z).
Axes of the slice: x: 4, y: 8, z: 8, core: 2. Of those that a mesh axis runs over, the one named last changes fastest.
Arguments:
- query: bfloat16 [512, 8192], P(('dp', 'seq'), 'tensor'), may hold values from -40 to 40
- fresh_key_value: bfloat16 [512, 2, 1024], P(('dp', 'seq'), None, 'tensor'), may hold values from -6 to 6
- cache: bfloat16 [512, 256, 2, 1024], P(('dp', 'seq'), None, None, 'tensor'), may hold values from -20 to 20
- lengths: int32 [512], P(('dp', 'seq')), may hold values from 2 to 256
- destination: int32 [512, 1], P(('dp', 'tensor')), may hold values from 0 to 32; in each aligned block of 32 rows (0 to 31, 32 to 63, ...) at most 2 rows name the same one
- out_weight: bfloat16 [8192, 8192], P('tensor', 'seq'), may hold values from -0.0625 to 0.0625
- learner_ctx: bfloat16 [8192, 8192], P(('dp', 'seq'), 'tensor'), may hold values from -6 to 6
Outputs:
- decoded: bfloat16 [512, 8192], P(('dp', 'tensor'), 'seq')
- handed: bfloat16 [2, 32, 8, 2, 8192], P('dp', 'seq', 'tensor')
- recomputed: bfloat16 [8192, 8192], P(('dp', 'tensor'), 'seq')
Inputs may be any that keep to these rules, and one draw needn't show every extreme that they name: In each block of 32 projected rows no destination is named by more than 2 rows, and some destination reaches 2.
All inputs are finite; a program needn't handle non-finite values.
Results may differ from a plain program's by a relative error of at most 0.017.
Values may be sent and summed in bfloat16 or wider, within the bound.
A program may use at most 64 MiB of HBM per device.

v0:
```python
import jax
import jax.numpy as jnp
from jax import lax
from jax.sharding import PartitionSpec as P

QUERY_HEADS = 64
KEY_VALUE_HEADS = 8
HEAD_SIZE = 128
CACHED_POSITIONS = 256


def attend_local(query, fresh_key_value, cache, lengths):
    row_count = query.shape[0]
    heads_kv = cache.shape[3] // HEAD_SIZE
    query_group = QUERY_HEADS // KEY_VALUE_HEADS
    score_scale = HEAD_SIZE ** (-0.5)
    head_list = query.reshape(row_count, heads_kv, query_group, HEAD_SIZE)
    rows_of_keys = cache[:, :, 0].reshape(row_count, CACHED_POSITIONS, heads_kv, HEAD_SIZE)
    rows_of_values = cache[:, :, 1].reshape(row_count, CACHED_POSITIONS, heads_kv, HEAD_SIZE)
    self_key = fresh_key_value[:, 0].reshape(row_count, heads_kv, HEAD_SIZE)
    self_value = fresh_key_value[:, 1].reshape(row_count, heads_kv, HEAD_SIZE)
    scores = (
        jnp.einsum("rgjd,rpgd->rgjp", head_list, rows_of_keys, preferred_element_type=jnp.float32)
        * score_scale
    )
    own = (
        jnp.einsum("rgjd,rgd->rgj", head_list, self_key, preferred_element_type=jnp.float32)
        * score_scale
    )
    valid = jnp.arange(CACHED_POSITIONS)[None, :] < lengths[:, None]
    scores = jnp.where(valid[:, None, None, :], scores, -jnp.inf)
    top = jnp.maximum(jnp.max(scores, axis=-1), own)
    expd = jnp.exp(scores - top[..., None])
    own_exp = jnp.exp(own - top)
    total = jnp.sum(expd, axis=-1) + own_exp
    weights = (expd / total[..., None]).astype(jnp.bfloat16)
    own_weight = (own_exp / total).astype(jnp.bfloat16)
    context = jnp.einsum(
        "rgjp,rpgd->rgjd", weights, rows_of_values, preferred_element_type=jnp.float32
    )
    context = (
        context
        + own_weight.astype(jnp.float32)[..., None] * self_value.astype(jnp.float32)[:, :, None, :]
    )
    return context.reshape(row_count, heads_kv * query_group * HEAD_SIZE).astype(jnp.bfloat16)


def local(query, fresh_key_value, cache, lengths, destination, out_weight, learner_ctx):
    context = attend_local(query, fresh_key_value, cache, lengths)
    gathered_ctx = lax.all_gather(context, "seq", axis=0, tiled=True)
    learn_terms = jnp.dot(
        lax.all_gather(learner_ctx, "seq", axis=0, tiled=True),
        out_weight,
        preferred_element_type=jnp.float32,
    )
    decode_terms = jnp.dot(gathered_ctx, out_weight, preferred_element_type=jnp.float32)
    decoded = lax.psum_scatter(decode_terms, "tensor", scatter_dimension=0, tiled=True).astype(
        jnp.bfloat16
    )
    recomputed = lax.psum_scatter(
        learn_terms.astype(jnp.bfloat16), "tensor", scatter_dimension=0, tiled=True
    )
    seq_count = lax.axis_size("seq")
    block_rows = decoded.shape[0]
    slot_count = max(2, block_rows // seq_count + 1)
    target = destination[:, 0]
    onehot = (target[:, None] == jnp.arange(seq_count)[None, :]).astype(jnp.int32)
    ranks = jnp.cumsum(onehot, axis=0) - 1
    placed = (ranks[:, :, None] == jnp.arange(slot_count)[None, None, :]) & (
        onehot[:, :, None] == 1
    )
    placement_map = (
        jnp.transpose(placed, (1, 2, 0))
        .reshape(seq_count * slot_count, block_rows)
        .astype(jnp.bfloat16)
    )
    outgoing = jnp.dot(placement_map, decoded, preferred_element_type=jnp.float32).astype(
        jnp.bfloat16
    )
    outgoing = outgoing.reshape(seq_count, slot_count, decoded.shape[1])
    arrived = lax.all_to_all(outgoing, "seq", split_axis=0, concat_axis=2, tiled=True)
    handed = arrived.reshape(1, 1, 1, slot_count, arrived.shape[2])
    return (decoded, handed, recomputed)


def solution(mesh):
    return jax.shard_map(
        local,
        mesh=mesh,
        in_specs=(
            P(("dp", "seq"), "tensor"),
            P(("dp", "seq"), None, "tensor"),
            P(("dp", "seq"), None, None, "tensor"),
            P(("dp", "seq")),
            P(("dp", "tensor"), None),
            P("tensor", "seq"),
            P(("dp", "seq"), "tensor"),
        ),
        out_specs=(
            P(("dp", "tensor"), "seq"),
            P("dp", "seq", "tensor", None, None),
            P(("dp", "tensor"), "seq"),
        ),
        check_vma=False,
    )
```

profile of v0, /device:TPU:6, one launch (start us, length us, event | category | flops | bytes accessed | tf_op | source)
XLA Modules:
  0.0 179.2 jit_solution(5482980129499225535)
XLA Ops:
  8.0 0.0 copy-start
  8.0 0.0 all-gather.2.cloned.1.call-start
  8.1 0.7 all-gather.2.cloned.1.call-update
  8.7 0.0 reduce-scatter.3.cloned.1.call-start
  8.8 0.8 slice_convert_fusion
  9.6 0.7 iota_compare_fusion.2
  10.3 0.8 fusion.10
  11.1 3.4 %fusion.16 = (bf16[8,256,1,128]{3,2,1,0:T(2,128)(2,1)S(1)}, bf16[8,256,1,128]{3,2,1,0:T(2,128)(2,1)S(1)}) fusion(bf16[8,256,2,128]{3,2,1,0:T(2,128)(2,1)} %param.9), kind=kLoop, calls=%fused_computation.35 | loop fusion | bytes 2097152 | tf_op jit(solution)/shard_map/slice | solution.py:18
  14.5 1.0 fusion.17
  15.6 0.2 fusion.3
  15.8 0.2 fusion.2
  16.0 52.5 %all_gather.6 = bf16[256,1024]{1,0:T(8,128)(2,1)S(1)} all-gather(bf16[8,1024]{1,0:T(8,128)(2,1)S(1)} %bitcast.37), channel_id=1, replica_groups=mesh['dp'=2,'seq'=32,'tensor'=8] {'seq'}, dimensions={0}, use_global_device_ids=true | all-gather | bytes 540672 | tf_op jit(solution)/shard_map/all_gather | solution.py:50
  68.5 0.0 copy-done
  68.5 1.0 fusion.18
  69.5 0.0 reduce-scatter.3.cloned.1.call-update
  69.5 0.0 copy-start.2
  69.6 0.0 reduce-scatter.5.cloned.1.call-start
  69.6 49.5 %all-gather.2.cloned.1.call-done = bf16[4096,1024]{1,0:T(8,128)(2,1)} async-done(((bf16[128,1024]{1,0:T(8,128)(2,1)}), bf16[4096,1024]{1,0:T(8,128)(2,1)}) %all-gather.2.cloned.1.call-update) | async-done | bytes 8388624 | tf_op jit(solution)/shard_map/all_gather | solution.py:52
  119.1 7.1 %convolution_convert_fusion = bf16[4096,256]{1,0:T(8,128)(2,1)} fusion(bf16[4096,1024]{1,0:T(8,128)(2,1)} %all-gather.2.cloned.1.call-done, bf16[1024,256]{1,0:T(8,128)(2,1)S(1)} %copy-done), kind=kOutput, calls=%fused_computation | convolution fusion | flops 2148532224 | bytes 11010048 | tf_op jit(solution)/shard_map/dot_general | solution.py:51
  126.2 0.0 reduce-scatter.5.cloned.1.call-update
  126.3 0.1 eq.67
  126.4 0.0 copy-done.2
  126.4 0.1 fusion.9
  126.4 0.1 reduce_window_sum.11
  126.5 0.1 copy.19
  126.6 0.0 reduce-scatter.3.cloned.1.call-done
  126.7 0.8 convert_element_type.48
  127.4 0.0 copy-start.1
  127.5 0.2 convolution_convert_fusion.1
  127.7 15.8 %all_to_all.15 = bf16[32,2,256]{2,1,0:T(2,128)(2,1)S(1)} all-to-all(bf16[32,2,256]{2,1,0:T(2,128)(2,1)S(1)} %reshape.154), channel_id=1, replica_groups=mesh['dp'=2,'seq'=32,'tensor'=8] {'seq'}, dimensions={0} | all-to-all | bytes 65536 | tf_op jit(solution)/shard_map/all_to_all | solution.py:81
  143.5 27.7 %reduce-scatter.5.cloned.1.call-done = bf16[512,256]{1,0:T(8,128)(2,1)} async-done(((bf16[4096,256]{1,0:T(8,128)(2,1)}), bf16[512,256]{1,0:T(8,128)(2,1)}) %reduce-scatter.5.cloned.1.call-update) | async-done | bytes 262160 | tf_op jit(solution)/shard_map/reduce_scatter | solution.py:60
  171.2 0.6 copy.47
  171.8 0.0 copy-done.1
  (10 shorter events, 0.1 us)
Async XLA Ops:
  8.0 60.5 %copy-start = (bf16[1024,256]{1,0:T(8,128)(2,1)S(1)}, bf16[1024,256]{1,0:T(8,128)(2,1)}, u32[]{:S(2)}) copy-start(bf16[1024,256]{1,0:T(8,128)(2,1)} %param.12) | copy-start | bytes 1572868
  8.0 111.1 %all-gather.2.cloned.1.call-start = ((), (), s32[]{:S(2)}) async-start(), calls=%async_computation.4 | async-start | bytes 8650752 | tf_op jit(solution)/shard_map/all_gather | solution.py:52
  8.7 117.9 %reduce-scatter.3.cloned.1.call-start = ((), (), s32[]{:S(2)}) async-start(), calls=%async_computation.3 | async-start | bytes 294912 | tf_op jit(solution)/shard_map/reduce_scatter | solution.py:57
  69.5 56.8 %copy-start.2 = (s32[32,1]{0,1:T(1,128)S(1)}, s32[32,1]{0,1:T(1,128)}, u32[]{:S(2)}) copy-start(s32[32,1]{0,1:T(1,128)} %param.11) | copy-start | bytes 388
  69.6 101.6 %reduce-scatter.5.cloned.1.call-start = ((), (), s32[]{:S(2)}) async-start(), calls=%async_computation.5 | async-start | bytes 2359296 | tf_op jit(solution)/shard_map/reduce_scatter | solution.py:60
  127.4 44.3 %copy-start.1 = (bf16[32,256]{1,0:T(8,128)(2,1)}, bf16[32,256]{1,0:T(8,128)(2,1)S(1)}, u32[]{:S(2)}) copy-start(bf16[32,256]{1,0:T(8,128)(2,1)S(1)} %convert_element_type.48) | copy-start | bytes 49156
Sparse Core Ops, SparseCore 0:
  12.5 106.5 all-gather.1
Sparse Core Ops, SparseCore 1:
  69.6 39.9 reduce-scatter.2
  126.3 44.8 reduce-scatter.4
where the time goes:
time: 180 us; the launch traced here: 179 us
  waiting for transfers between devices  77.9 us (43%)
  blocking collectives  68.3 us (38%)
  between operations  15.6 us (9%)
  matrix products  10.4 us (6%)
  local copies, waits for them, and re-layouts  4.29 us (2%)
  other arithmetic  2.6 us (1%)
    all_gather x1, blocking collectives, local(): gathered_ctx = lax.all_gather(context, 'seq', axis=0, tiled=True)  52.5 us
    all_gather x1, waiting for transfers between devices, local(): lax.all_gather(learner_ctx, 'seq', axis=0, tiled=True)  49.5 us
    reduce_scatter x1, waiting for transfers between devices, local(): lax.psum_scatter(learn_terms.astype(jnp.bfloat16), 'tensor', scatter_dime...  27.7 us
    all_to_all x1, blocking collectives, local(): lax.all_to_all(outgoing, 'seq', split_axis=0, concat_axis=2, tiled=True)  15.8 us
    dot_general x1, matrix products, local(): jnp.dot(lax.all_gather(learner_ctx, 'seq', axis=0, tiled=True), out_weigh...  7.1 us
  transfers between devices with their start and end apart: 3, of which 2 were waited for; matrix products, arithmetic and copies ran while one was open for 9% of the time, Pallas kernels for 0%

commit v1 on v0

v1 whole, which is shorter than its diff:
```python
import jax
import jax.numpy as jnp
from jax import lax
from jax.experimental import pallas as pl
from jax.experimental.pallas import tpu as pltpu
from jax.sharding import PartitionSpec as P

QUERY_GROUP = 8
HEAD_SIZE = 128
CACHED_POSITIONS = 256
NX, NY, NZ = 4, 8, 8
BLOCK = 128
HALF = 64
WIDTH = 1024
COLS = 256
ITEMS = NY
SLOTS = ITEMS + NZ - 1
OFFSETS = (0, 3, 1, 2)
MESH_ID = pl.DeviceIdType.MESH
BF16, F32 = jnp.bfloat16, jnp.float32


def dot(a, b):
    return jnp.dot(a, b, preferred_element_type=F32)


def dot_t(a, b):
    return lax.dot_general(a, b, (((1,), (1,)), ((), ())), preferred_element_type=F32)


def iota(shape, dim):
    return lax.broadcasted_iota(jnp.int32, shape, dim)


def one_hot(condition):
    return jnp.where(condition, 1.0, 0.0).astype(BF16)


def attend(q_ref, f_ref, c_ref, len_ref):
    rows = 8
    by_head = jnp.concatenate(
        [q_ref[:, h * HEAD_SIZE : (h + 1) * HEAD_SIZE].astype(F32) for h in range(QUERY_GROUP)], axis=0
    ).astype(BF16)
    r64, c64 = iota((64, 64), 0), iota((64, 64), 1)
    swap = one_hot((r64 % 8) * 8 + r64 // 8 == c64)
    queries = dot(swap, by_head)
    scale = HEAD_SIZE ** (-0.5)
    scores = []
    place = iota((8, 2 * CACHED_POSITIONS), 1)
    for r in range(rows):
        s = dot_t(queries[r * 8 : (r + 1) * 8].astype(BF16), c_ref[r]) * scale
        valid = (place % 2 == 0) & (place < 2 * len_ref[r])
        scores.append(jnp.where(valid, s, -1e30))
    scores = jnp.concatenate(scores, axis=0)
    fresh = f_ref[...]
    fresh_scores = dot_t(queries.astype(BF16), fresh) * scale
    row16, col16 = iota((64, 16), 0), iota((64, 16), 1)
    own = jnp.sum(jnp.where(col16 == 2 * (row16 // 8), fresh_scores, 0.0), axis=1, keepdims=True)
    top = jnp.maximum(jnp.max(scores, axis=1, keepdims=True), own)
    expd = jnp.exp(scores - top)
    own_exp = jnp.exp(own - top)
    total = jnp.sum(expd, axis=1, keepdims=True) + own_exp
    weights = pltpu.roll(expd / total, 1, 1)
    own_weight = jnp.where(col16 == 2 * (row16 // 8) + 1, own_exp / total, 0.0).astype(BF16)
    context = [dot(weights[r * 8 : (r + 1) * 8].astype(BF16), c_ref[r]) for r in range(rows)]
    context = jnp.concatenate(context, axis=0) + dot(own_weight, fresh)
    context = dot(swap, context.astype(BF16))
    halves = [
        jnp.concatenate([context[h * 8 : (h + 1) * 8] for h in range(g * 4, g * 4 + 4)], axis=1) for g in (0, 1)
    ]
    return jnp.concatenate(halves, axis=0).astype(BF16)


def placement(dest_ref):
    dest = dest_ref[...].astype(F32)
    r32, c32 = iota((32, 32), 0), iota((32, 32), 1)
    across = jnp.broadcast_to(dest, (32, 32))
    down = dot(jnp.where(r32 == c32, across, 0.0).astype(BF16), jnp.ones((32, 32), BF16))
    earlier = one_hot((down == across) & (r32 < c32))
    rank = dot(jnp.ones((128, 32), BF16), earlier)
    q, i = iota((128, 32), 0), iota((128, 32), 1)
    target = ((q // 4) % 4) * NY + q // 16
    slot = (q // 2) % 2
    hit = (jnp.broadcast_to(dest, (128, 32)) == target.astype(F32)) & (rank == slot.astype(F32))
    return [one_hot(hit & (q % 2 == h)) for h in (0, 1)]


def regroup():
    r, c = iota((128, 128), 0), iota((128, 128), 1)
    return one_hot((r // 4 % 8) * 16 + (r // 32) * 4 + r % 4 == c)


def regroup_last():
    r, c = iota((128, 128), 0), iota((128, 128), 1)
    return one_hot((r // 2 % 32) * 4 + (r // 64) * 2 + r % 2 == c)


def kernel(
    q_ref, f_ref, c_ref, len_ref, dest_ref, w_ref, a_ref,
    dec_ref, hand_ref, rec_ref,
    abuf, wbuf, pbuf, rbuf, sbuf, cbuf, zs, zr, h1s, h1r, h2s, h2r,
    a_send, a_recv, w_send, w_recv, d_send, d_recv, c_send, c_recv, out_recv,
):
    core, seq, z = lax.axis_index("dp"), lax.axis_index("seq"), lax.axis_index("tensor")
    x, y = seq // NY, seq % NY

    def at(dx=0, dy=0, dz=0):
        return {"seq": lax.rem(x + dx + NX, NX) * NY + lax.rem(y + dy + NY, NY), "tensor": lax.rem(z + dz + NZ, NZ)}

    sibling = {"dp": 1 - core}
    partners = (
        [at(dx=k) for k in range(1, NX)] + [at(dy=k) for k in range(1, NY)] + [at(dz=k) for k in range(1, NZ)] + [sibling]
    )

    def send(src, dst, send_sem, recv_sem, device):
        copy = pltpu.make_async_remote_copy(
            src_ref=src, dst_ref=dst, send_sem=send_sem, recv_sem=recv_sem, device_id=device, device_id_type=MESH_ID
        )
        copy.start()

    def wait(ref, sem):
        pltpu.make_async_copy(ref, ref, sem).wait()

    barrier = pltpu.get_barrier_semaphore()
    for device in partners:
        pl.semaphore_signal(barrier, inc=1, device_id=device, device_id_type=MESH_ID)
    abuf[0] = a_ref[...]
    pl.semaphore_wait(barrier, len(partners))

    def half(item, h):
        return abuf.at[item, pl.ds(pl.multiple_of(h * HALF, HALF), HALF)]

    def send_rows(stream, source, target, h):
        send(half(source, h), half(target, h), a_send.at[stream], a_recv.at[stream, target - 1], at(dy=1 - 2 * stream))

    for i in (0, 1):
        for stream in (0, 1):
            send_rows(stream, 0, i + 1, (i + stream) % 2)

    kept = pl.multiple_of(core * (WIDTH // 2), WIDTH // 2)
    mine, other = pl.ds(kept, WIDTH // 2), pl.ds(pl.multiple_of(WIDTH // 2 - kept, WIDTH // 2), WIDTH // 2)
    quarter = [pl.ds(pl.multiple_of(kept + k * (WIDTH // 4), WIDTH // 4), WIDTH // 4) for k in (0, 1)]
    send(w_ref.at[mine], wbuf.at[0, mine], w_send.at[0], w_recv.at[0], at(dx=1))
    send(w_ref.at[mine], wbuf.at[1, mine], w_send.at[0], w_recv.at[1], at(dx=-1))

    cbuf[x, y] = attend(q_ref, f_ref, c_ref, len_ref)
    for k in range(1, NY):
        send(cbuf.at[x, y], cbuf.at[x, y], d_send.at[0], d_recv.at[0], at(dy=k))

    def gather(i):
        for stream in (0, 1):
            h = lax.rem(i + stream, 2)
            wait(half(i + 1, h), a_recv.at[stream, i])

            @pl.when(i < 5)
            def _():
                send_rows(stream, i + 1, i + 3, h)

    gather(0)
    for k in (0, 1):
        wait(wbuf.at[k, mine], w_recv.at[k])
        send(wbuf.at[k, quarter[k]], wbuf.at[2, quarter[k]], w_send.at[0], w_recv.at[2 + k], at(dx=1 - 2 * k))
        send(wbuf.at[k, mine], wbuf.at[k, mine], w_send.at[1], w_recv.at[4 + k], sibling)
    gather(1)
    wait(cbuf.at[x, pl.ds(0, NY - 1)], d_recv.at[0])
    for k in range(1, NX):
        send(cbuf.at[x], cbuf.at[x], d_send.at[1], d_recv.at[1], at(dx=k))
    gather(2)
    for k in (0, 1):
        wait(wbuf.at[2, quarter[k]], w_recv.at[2 + k])
    send(wbuf.at[2, mine], wbuf.at[2, mine], w_send.at[1], w_recv.at[6], sibling)
    for j in range(3):
        wait(wbuf.at[j, other], w_recv.at[4 + j])

    def chain(s, way, root):
        tz = 2 * x + root
        place = lax.rem(z - tz - 1 + 2 * NZ, NZ) if way == 0 else lax.rem(tz - 1 - z + 2 * NZ, NZ)
        m = s - place
        k = (m + 1) // 2
        item_y = lax.rem(y + 2 * NY + jnp.where(lax.rem(m + 1 + NZ, 2) == way, -k, k), NY)

        @pl.when((m >= 0) & (m < ITEMS) & (item_y // 4 == root))
        def _():
            for j in range(NX):
                own = pbuf.at[m, j, pl.ds(way * HALF, HALF)]

                @pl.when(place == 0)
                def _():
                    sbuf[way, m, j] = own[...].astype(BF16)

                @pl.when(place > 0)
                def _():
                    wait(rbuf.at[way, m, j], c_recv.at[way, m, j])
                    sbuf[way, m, j] = (own[...] + rbuf[way, m, j].astype(F32)).astype(BF16)

                @pl.when(place < NZ - 1)
                def _():
                    send(
                        sbuf.at[way, m, j], rbuf.at[way, m, j], c_send.at[way], c_recv.at[way, m, j],
                        at(dz=1 - 2 * way),
                    )

                @pl.when(place == NZ - 1)
                def _():
                    rows = pl.ds(pl.multiple_of(lax.rem(item_y, 4) * BLOCK + way * HALF, HALF), HALF)
                    if j == 0:
                        pltpu.make_async_copy(sbuf.at[way, m, j], rec_ref.at[rows], c_send.at[way]).start()
                    else:
                        send(sbuf.at[way, m, j], rec_ref.at[rows], c_send.at[way], out_recv.at[0], at(dx=OFFSETS[j]))

    def project_decode():
        wait(cbuf.at[pl.ds(0, NX - 1)], d_recv.at[1])
        for g in range(NX):
            rows = cbuf[g].reshape(NY * 16, 512)
            low = dot(rows, w_ref[0:512]).reshape(NY, 16, COLS)
            high = dot(rows, w_ref[512:1024]).reshape(NY, 16, COLS)
            zs[2 * g : 2 * g + 2] = (low[:, :8] + high[:, 8:]).reshape(2, 32, COLS).astype(BF16)
        zr[z] = zs[z]
        for k in range(1, NZ):
            send(zs.at[lax.rem(z + k, NZ)], zr.at[z], d_send.at[2], d_recv.at[2], at(dz=k))

    def hand_over():
        wait(zr.at[pl.ds(0, NZ - 1)], d_recv.at[2])
        total = zr[0].astype(F32)
        for k in range(1, NZ):
            total = total + zr[k].astype(F32)
        decoded = total.astype(BF16)
        dec_ref[...] = decoded
        maps = placement(dest_ref)
        out = dot(maps[0], decoded[:, :128]) + dot(maps[1], decoded[:, 128:])
        h1s[...] = out.astype(BF16).reshape(NY, 16, 128)
        h1r[y] = h1s[y]
        for k in range(1, NY):
            send(h1s.at[lax.rem(y + k, NY)], h1r.at[y], d_send.at[3], d_recv.at[3], at(dy=k))

    def hand_on():
        wait(h1r.at[pl.ds(0, NY - 1)], d_recv.at[3])
        h2s[...] = dot(regroup(), h1r[...].reshape(128, 128)).astype(BF16).reshape(NX, 32, 128)
        h2r[x] = h2s[x]
        for k in range(1, NX):
            send(h2s.at[lax.rem(x + k, NX)], h2r.at[x], d_send.at[4], d_recv.at[4], at(dx=k))

    def take():
        wait(h2r.at[pl.ds(0, NX - 1)], d_recv.at[4])
        hand_ref[...] = dot(regroup_last(), h2r[...].reshape(128, 128)).astype(BF16)

    def slot(s, carry):
        @pl.when((s >= 4) & (s < ITEMS))
        def _():
            gather(s - 1)

        @pl.when(s < ITEMS)
        def _():
            rows = abuf[s]
            for j in range(NX):
                pbuf[s, j] = dot(rows, w_ref[...] if j == 0 else wbuf[j - 1])

        for way in (0, 1):
            for root in (0, 1):
                chain(s, way, root)
        for step, task in ((3, project_decode), (5, hand_over), (7, hand_on), (9, take)):
            pl.when(s == step)(task)
        return carry

    lax.fori_loop(0, SLOTS, slot, 0)

    @pl.when(x != z // 2)
    def _():
        wait(rec_ref, out_recv.at[0])

    for way in (0, 1):
        wait(sbuf.at[way], c_send.at[way])
        wait(abuf.at[pl.ds(0, 7), pl.ds(0, HALF)], a_send.at[way])
    wait(wbuf.at[pl.ds(0, 2), mine], w_send.at[0])
    for k in (0, 1):
        wait(wbuf.at[k, quarter[k]], w_send.at[0])
    wait(wbuf.at[:, mine], w_send.at[1])
    wait(cbuf.at[0, pl.ds(0, NY - 1)], d_send.at[0])
    wait(cbuf.at[pl.ds(0, NX - 1)], d_send.at[1])
    wait(zs.at[pl.ds(0, NZ - 1)], d_send.at[2])
    wait(h1s.at[pl.ds(0, NY - 1)], d_send.at[3])
    wait(h2s.at[pl.ds(0, NX - 1)], d_send.at[4])


def local(query, fresh_key_value, cache, lengths, destination, out_weight, learner_ctx):
    vmem = pl.BlockSpec(memory_space=pltpu.VMEM)
    dma = pltpu.SemaphoreType.DMA
    decoded, handed, recomputed = pl.pallas_call(
        kernel,
        out_shape=(
            jax.ShapeDtypeStruct((32, COLS), BF16),
            jax.ShapeDtypeStruct((128, 128), BF16),
            jax.ShapeDtypeStruct((512, COLS), BF16),
        ),
        in_specs=[vmem, vmem, vmem, pl.BlockSpec(memory_space=pltpu.SMEM), vmem, vmem, vmem],
        out_specs=(vmem, vmem, vmem),
        scratch_shapes=[
            pltpu.VMEM((ITEMS, BLOCK, WIDTH), BF16),
            pltpu.VMEM((NX - 1, WIDTH, COLS), BF16),
            pltpu.VMEM((ITEMS, NX, BLOCK, COLS), F32),
            pltpu.VMEM((2, ITEMS, NX, HALF, COLS), BF16),
            pltpu.VMEM((2, ITEMS, NX, HALF, COLS), BF16),
            pltpu.VMEM((NX, NY, 16, 512), BF16),
            pltpu.VMEM((NZ, 32, COLS), BF16),
            pltpu.VMEM((NZ, 32, COLS), BF16),
            pltpu.VMEM((NY, 16, 128), BF16),
            pltpu.VMEM((NY, 16, 128), BF16),
            pltpu.VMEM((NX, 32, 128), BF16),
            pltpu.VMEM((NX, 32, 128), BF16),
            dma((2,)),
            dma((2, 7)),
            dma((2,)),
            dma((7,)),
            dma((5,)),
            dma((5,)),
            dma((2,)),
            dma((2, ITEMS, NX)),
            dma((1,)),
        ],
        compiler_params=pltpu.CompilerParams(
            collective_id=0, has_side_effects=True, vmem_limit_bytes=48 * 1024 * 1024
        ),
        cost_estimate=pl.CostEstimate(flops=2300000000, bytes_accessed=2500000, transcendentals=33000),
        name="project",
    )(
        query,
        fresh_key_value.reshape(16, HEAD_SIZE),
        cache.reshape(8, 2 * CACHED_POSITIONS, HEAD_SIZE),
        lengths,
        destination.reshape(1, 32),
        out_weight,
        learner_ctx,
    )
    return decoded, handed.reshape(1, 1, 1, 2, 8192), recomputed


def solution(mesh):
    return jax.shard_map(
        local,
        mesh=mesh,
        in_specs=(
            P(("dp", "seq"), "tensor"),
            P(("dp", "seq"), None, "tensor"),
            P(("dp", "seq"), None, None, "tensor"),
            P(("dp", "seq")),
            P(("dp", "tensor"), None),
            P("tensor", "seq"),
            P(("dp", "seq"), "tensor"),
        ),
        out_specs=(
            P(("dp", "tensor"), "seq"),
            P("dp", "seq", "tensor", None, None),
            P(("dp", "tensor"), "seq"),
        ),
        check_vma=False,
    )
```

time: 180 us -> 96.6 us (0.54)
  Pallas kernels: 0 us -> 89.1 us
  waiting for transfers between devices: 77.9 us -> 0 us
  blocking collectives: 68.3 us -> 0 us
  between operations: 15.6 us -> 0.67 us
  matrix products: 10.4 us -> 0 us
  other arithmetic: 2.6 us -> 0 us
  local copies, waits for them, and re-layouts: 4.29 us -> 6.54 us
    pallas_call x0 -> x1, Pallas kernels: none -> 89.1 us  [local(): pl.pallas_call(kernel, out_shape=(jax.ShapeDtypeStruct((32, COLS), BF16),...]
    all_gather x1 -> x0, blocking collectives: 52.5 us -> none  [local(): gathered_ctx = lax.all_gather(context, 'seq', axis=0, tiled=True)]
    all_gather x1 -> x0, waiting for transfers between devices: 49.5 us -> none  [local(): lax.all_gather(learner_ctx, 'seq', axis=0, tiled=True)]
    reduce_scatter x2 -> x0, waiting for transfers between devices: 27.7 us -> none  [the longest x1 27.7 us: local(): lax.psum_scatter(learn_terms.astype(jnp.bfloat16), 'tensor', scatter_dime...]
    all_to_all x1 -> x0, blocking collectives: 15.8 us -> none  [local(): lax.all_to_all(outgoing, 'seq', split_axis=0, concat_axis=2, tiled=True)]
    dot_general x6 -> x0, matrix products: 10.4 us -> none  [the longest x1 7.1 us: local(): jnp.dot(lax.all_gather(learner_ctx, 'seq', axis=0, tiled=True), out_weigh...]
    unnamed x9 -> x16, local copies, waits for them, and re-layouts: 0.65 us -> 5.91 us
    slice x1 -> x0, local copies, waits for them, and re-layouts: 3.38 us -> none  [attend_local(): cache[:, :, 0].reshape(row_count, CACHED_POSITIONS, heads_kv, HEAD_SIZE)]
  transfers between devices with their start and end apart: 3 -> 0, of which waited for: 2 -> 0; matrix products, arithmetic and copies ran while one was open for 9% -> 0% of each run, Pallas kernels for 0% -> 0%
where the time goes in v1:
time: 96.6 us; the launch traced here: 96.3 us
  Pallas kernels  89.1 us (92%)
  local copies, waits for them, and re-layouts  6.54 us (7%)
    pallas_call x1, Pallas kernels, local(): pl.pallas_call(kernel, out_shape=(jax.ShapeDtypeStruct((32, COLS), BF16),...  89.1 us
    unnamed x16, local copies, waits for them, and re-layouts  5.91 us

profile of v1, /device:TPU:6, one launch (start us, length us, event | category | flops | bytes accessed | tf_op | source)
XLA Modules:
  0.0 96.3 jit_solution(18219487618198201602)
XLA Ops:
  0.6 0.0 copy-start.4
  0.6 0.0 copy-start.5
  0.7 0.0 copy-start.6
  0.7 0.7 copy-done.4
  1.3 0.0 copy-done.5
  1.3 0.0 copy-done.6
  1.3 0.0 copy-start
  1.3 1.2 %copy-done = bf16[8,256,2,128]{3,2,1,0:T(2,128)(2,1)S(1)} copy-done((bf16[8,256,2,128]{3,2,1,0:T(2,128)(2,1)S(1)}, bf16[8,256,2,128]{3,2,1,0:T(2,128)(2,1)}, u32[]{:S(2)}) %copy-start) | copy-done | bytes 1048600
  2.6 0.0 copy-start.1
  2.6 1.0 %copy-done.1 = bf16[1024,256]{1,0:T(8,128)(2,1)S(1)} copy-done((bf16[1024,256]{1,0:T(8,128)(2,1)S(1)}, bf16[1024,256]{1,0:T(8,128)(2,1)}, u32[]{:S(2)}) %copy-start.1) | copy-done | bytes 524312
  3.6 0.0 copy-start.2
  3.6 0.9 copy-done.2
  4.5 0.0 copy-start.3
  4.5 0.7 copy-done.3
  5.3 89.1 %project.1 = (bf16[32,256]{1,0:T(8,128)(2,1)S(1)}, bf16[128,128]{1,0:T(8,128)(2,1)S(1)}, bf16[512,256]{1,0:T(8,128)(2,1)S(1)}) custom-call(bf16[8,1024]{1,0:T(8,128)(2,1)S(1)} %copy-done.3, bf16[16,128]{1,0:T(8,128)(2,1)S(1)} %bitcast.4, bf16[8,512,128]{2,1,0:T(8,128)(2,1)S(1)} %bitcast.3, s32[8]{0:T(128)S(1)} %copy-done.5, s32[1,32]{1,0:T(1,128)S(1)} %bitcast.5, ...), custom_call_target="tpu_custom_call" | custom-call | flops 2300000000 | bytes 2500000 | tf_op jit(solution)/shard_map/project/pallas_call | solution.py:288
  94.3 0.6 reshape.21
  95.0 0.6 copy.12
  95.6 0.7 copy.13
Async XLA Ops:
  0.6 0.7 copy-start.4
  0.6 0.7 copy-start.5
  0.7 0.7 copy-start.6
  1.3 1.2 %copy-start = (bf16[8,256,2,128]{3,2,1,0:T(2,128)(2,1)S(1)}, bf16[8,256,2,128]{3,2,1,0:T(2,128)(2,1)}, u32[]{:S(2)}) copy-start(bf16[8,256,2,128]{3,2,1,0:T(2,128)(2,1)} %param.9) | copy-start | bytes 3145732
  2.6 1.0 %copy-start.1 = (bf16[1024,256]{1,0:T(8,128)(2,1)S(1)}, bf16[1024,256]{1,0:T(8,128)(2,1)}, u32[]{:S(2)}) copy-start(bf16[1024,256]{1,0:T(8,128)(2,1)} %w_ref.1) | copy-start | bytes 1572868
  3.6 0.9 copy-start.2
  4.5 0.7 copy-start.3

commit v2 on v1

--- a/solution.py
+++ b/solution.py
@@ -14,8 +14,9 @@
 WIDTH = 1024
 COLS = 256
 ITEMS = NY
-SLOTS = ITEMS + NZ - 1
-OFFSETS = (0, 3, 1, 2)
+CHUNKS = [(0, 0), (1, 0), (2, 0), (0, 1), (0, 2), (1, 1), (1, 2), (2, 1), (2, 2), (3, 0), (3, 1), (3, 2)]
+CHUNKS += [(m, 3) for m in range(4)] + [(m, j) for m in range(4, ITEMS) for j in range(NX)]
+ROUNDS = 8
 MESH_ID = pl.DeviceIdType.MESH
 BF16, F32 = jnp.bfloat16, jnp.float32
 
@@ -96,10 +97,11 @@
 
 
 def kernel(
-    q_ref, f_ref, c_ref, len_ref, dest_ref, w_ref, a_ref,
+    q_hbm, f_hbm, c_hbm, len_hbm, dest_hbm, w_hbm, a_hbm,
     dec_ref, hand_ref, rec_ref,
+    q_ref, f_ref, c_ref, len_ref, dest_ref,
     abuf, wbuf, pbuf, rbuf, sbuf, cbuf, zs, zr, h1s, h1r, h2s, h2r,
-    a_send, a_recv, w_send, w_recv, d_send, d_recv, c_send, c_recv, out_recv,
+    in_sem, a_send, a_recv, w_send, w_recv, d_send, d_recv, c_send, c_recv, f_send, out_recv,
 ):
     core, seq, z = lax.axis_index("dp"), lax.axis_index("seq"), lax.axis_index("tensor")
     x, y = seq // NY, seq % NY
@@ -124,7 +126,19 @@
     barrier = pltpu.get_barrier_semaphore()
     for device in partners:
         pl.semaphore_signal(barrier, inc=1, device_id=device, device_id_type=MESH_ID)
-    abuf[0] = a_ref[...]
+    loads = [
+        pltpu.make_async_copy(src, dst, in_sem.at[k])
+        for k, (src, dst) in enumerate(
+            [
+                (a_hbm, abuf.at[0]), (w_hbm, wbuf.at[:, pl.ds(0, COLS)]), (q_hbm, q_ref), (c_hbm, c_ref),
+                (f_hbm, f_ref), (len_hbm, len_ref), (dest_hbm, dest_ref),
+            ]
+        )
+    ]
+    for load in loads:
+        load.start()
+    for load in loads:
+        load.wait()
     pl.semaphore_wait(barrier, len(partners))
 
     def half(item, h):
@@ -137,83 +151,130 @@
         for stream in (0, 1):
             send_rows(stream, 0, i + 1, (i + stream) % 2)
 
-    kept = pl.multiple_of(core * (WIDTH // 2), WIDTH // 2)
-    mine, other = pl.ds(kept, WIDTH // 2), pl.ds(pl.multiple_of(WIDTH // 2 - kept, WIDTH // 2), WIDTH // 2)
-    quarter = [pl.ds(pl.multiple_of(kept + k * (WIDTH // 4), WIDTH // 4), WIDTH // 4) for k in (0, 1)]
-    send(w_ref.at[mine], wbuf.at[0, mine], w_send.at[0], w_recv.at[0], at(dx=1))
-    send(w_ref.at[mine], wbuf.at[1, mine], w_send.at[0], w_recv.at[1], at(dx=-1))
-
-    cbuf[x, y] = attend(q_ref, f_ref, c_ref, len_ref)
-    for k in range(1, NY):
-        send(cbuf.at[x, y], cbuf.at[x, y], d_send.at[0], d_recv.at[0], at(dy=k))
-
     def gather(i):
         for stream in (0, 1):
-            h = lax.rem(i + stream, 2)
+            h = (i + stream) % 2
             wait(half(i + 1, h), a_recv.at[stream, i])
-
-            @pl.when(i < 5)
-            def _():
+            if i < 5:
                 send_rows(stream, i + 1, i + 3, h)
 
-    gather(0)
-    for k in (0, 1):
-        wait(wbuf.at[k, mine], w_recv.at[k])
-        send(wbuf.at[k, quarter[k]], wbuf.at[2, quarter[k]], w_send.at[0], w_recv.at[2 + k], at(dx=1 - 2 * k))
-        send(wbuf.at[k, mine], wbuf.at[k, mine], w_send.at[1], w_recv.at[4 + k], sibling)
-    gather(1)
-    wait(cbuf.at[x, pl.ds(0, NY - 1)], d_recv.at[0])
-    for k in range(1, NX):
-        send(cbuf.at[x], cbuf.at[x], d_send.at[1], d_recv.at[1], at(dx=k))
-    gather(2)
-    for k in (0, 1):
-        wait(wbuf.at[2, quarter[k]], w_recv.at[2 + k])
-    send(wbuf.at[2, mine], wbuf.at[2, mine], w_send.at[1], w_recv.at[6], sibling)
-    for j in range(3):
-        wait(wbuf.at[j, other], w_recv.at[4 + j])
-
-    def chain(s, way, root):
-        tz = 2 * x + root
-        place = lax.rem(z - tz - 1 + 2 * NZ, NZ) if way == 0 else lax.rem(tz - 1 - z + 2 * NZ, NZ)
-        m = s - place
-        k = (m + 1) // 2
-        item_y = lax.rem(y + 2 * NY + jnp.where(lax.rem(m + 1 + NZ, 2) == way, -k, k), NY)
-
-        @pl.when((m >= 0) & (m < ITEMS) & (item_y // 4 == root))
+    part = [pl.ds(pl.multiple_of(core * (WIDTH // 2) + k * (WIDTH // 4), WIDTH // 4), WIDTH // 4) for k in (0, 1)]
+    away = pl.multiple_of((1 - core) * (WIDTH // 2), WIDTH // 2)
+    others = [pl.ds(pl.multiple_of(away + k * (WIDTH // 4), WIDTH // 4), WIDTH // 4) for k in (0, 1)]
+
+    def block(rows, j):
+        return wbuf.at[rows, pl.ds(j * COLS, COLS)]
+
+    def send_weights(turn):
+        for way in (0, 1):
+            rows = part[way ^ turn]
+            send(block(rows, 0), block(rows, 1 + way), w_send.at[0], w_recv.at[way, turn], at(dx=1 - 2 * way))
+
+    def pass_weights(turn):
+        for way in (0, 1):
+            rows = part[way ^ turn]
+            held = block(rows, 1 + way)
+            wait(held, w_recv.at[way, turn])
+            if turn == 0:
+                send(held, block(rows, 3), w_send.at[0], w_recv.at[2, way], at(dx=1 - 2 * way))
+            send(held, held, w_send.at[1], w_recv.at[3 + way, turn], sibling)
+
+    def pass_last_weights():
+        for way in (0, 1):
+            held = block(part[way], 3)
+            wait(held, w_recv.at[2, way])
+            send(held, held, w_send.at[1], w_recv.at[5, way], sibling)
+
+    def take_weights(way):
+        for turn in (0, 1):
+            k = way ^ turn if way < 2 else turn
+            wait(block(others[k], 1 + way), w_recv.at[3 + way, turn])
+
+    send_weights(0)
+    send_weights(1)
+
+    def project(first, items, blocks):
+        rows = abuf[first : first + items].reshape(items * BLOCK, WIDTH)
+        out = dot(rows, wbuf[:, blocks[0] * COLS : (blocks[-1] + 1) * COLS])
+        for m in range(items):
+            for j in blocks:
+                c = CHUNKS.index((first + m, j))
+                for h in (0, 1):
+                    pbuf[2 * c + h] = out[
+                        m * BLOCK + h * HALF : m * BLOCK + (h + 1) * HALF,
+                        (j - blocks[0]) * COLS : (j - blocks[0] + 1) * COLS,
+                    ]
+
+    up = 1 - 2 * core
+
+    def piece(r, far):
+        return pbuf[8 * r + lax.rem(z + far + NZ, NZ)]
+
+    def stage(r, t):
+        for side in (0, 1):
+            if side > t:
+                continue
+            way = up if side == 0 else -up
+            at_slot, from_slot = 4 * side + t - side, 4 * side + t - side - 1
+            total = piece(r, way * (4 - t))
+            if t > side:
+                wait(rbuf.at[r, from_slot], c_recv.at[r, from_slot])
+                total = total + rbuf[r, from_slot].astype(F32)
+            sbuf[r, at_slot] = total.astype(BF16)
+            send(sbuf.at[r, at_slot], rbuf.at[r, at_slot], c_send.at[0], c_recv.at[r, at_slot], at(dz=way))
+
+    own_half, own_chunk = lax.rem(z, 2), z // 2
+
+    def pick(values):
+        out = values[3]
+        for k in range(3):
+            out = jnp.where(own_chunk == k, values[k], out)
+        return out
+
+    def place(r):
+        chunks = CHUNKS[4 * r : 4 * r + 4]
+        j = pick([c[1] for c in chunks])
+        dx = jnp.where(j == 1, NX - 1, jnp.where(j == 0, 0, j - 1))
+        steps = pick([(c[0] + 1) // 2 for c in chunks])
+        sign = pick([1 if c[0] % 2 == 0 else -1 for c in chunks]) * (1 - 2 * own_half)
+        item_y = lax.rem(y + sign * steps + 2 * NY, NY)
+        dz = 2 * x + item_y // 4 - z
+        row = pl.multiple_of(lax.rem(item_y, 4) * BLOCK + own_half * HALF, HALF)
+        return dx, dz, row, (dx == 0) & (dz == 0)
+
+    def finish(r):
+        total = piece(r, 0)
+        for slot in (3, 6):
+            wait(rbuf.at[r, slot], c_recv.at[r, slot])
+            total = total + rbuf[r, slot].astype(F32)
+        sbuf[r, 7] = total.astype(BF16)
+        dx, dz, row, stays = place(r)
+        rows = rec_ref.at[pl.ds(row, HALF)]
+
+        @pl.when(stays)
         def _():
-            for j in range(NX):
-                own = pbuf.at[m, j, pl.ds(way * HALF, HALF)]
-
-                @pl.when(place == 0)
-                def _():
-                    sbuf[way, m, j] = own[...].astype(BF16)
-
-                @pl.when(place > 0)
-                def _():
-                    wait(rbuf.at[way, m, j], c_recv.at[way, m, j])
-                    sbuf[way, m, j] = (own[...] + rbuf[way, m, j].astype(F32)).astype(BF16)
-
-                @pl.when(place < NZ - 1)
-                def _():
-                    send(
-                        sbuf.at[way, m, j], rbuf.at[way, m, j], c_send.at[way], c_recv.at[way, m, j],
-                        at(dz=1 - 2 * way),
-                    )
-
-                @pl.when(place == NZ - 1)
-                def _():
-                    rows = pl.ds(pl.multiple_of(lax.rem(item_y, 4) * BLOCK + way * HALF, HALF), HALF)
-                    if j == 0:
-                        pltpu.make_async_copy(sbuf.at[way, m, j], rec_ref.at[rows], c_send.at[way]).start()
-                    else:
-                        send(sbuf.at[way, m, j], rec_ref.at[rows], c_send.at[way], out_recv.at[0], at(dx=OFFSETS[j]))
+            pltpu.make_async_copy(sbuf.at[r, 7], rows, out_recv.at[0]).start()
+
+        @pl.when(jnp.logical_not(stays))
+        def _():
+            send(sbuf.at[r, 7], rows, f_send.at[r], out_recv.at[0], at(dx=dx, dz=dz))
+
+    def send_context():
+        cbuf[x, y] = attend(q_ref, f_ref, c_ref, len_ref)
+        for k in range(1, NY):
+            send(cbuf.at[x, y], cbuf.at[x, y], d_send.at[0], d_recv.at[0], at(dy=k))
+
+    def pass_context():
+        wait(cbuf.at[x, pl.ds(0, NY - 1)], d_recv.at[0])
+        for k in range(1, NX):
+            send(cbuf.at[x], cbuf.at[x], d_send.at[1], d_recv.at[1], at(dx=k))
 
     def project_decode():
         wait(cbuf.at[pl.ds(0, NX - 1)], d_recv.at[1])
         for g in range(NX):
             rows = cbuf[g].reshape(NY * 16, 512)
-            low = dot(rows, w_ref[0:512]).reshape(NY, 16, COLS)
-            high = dot(rows, w_ref[512:1024]).reshape(NY, 16, COLS)
+            low = dot(rows, wbuf[0:512, 0:COLS]).reshape(NY, 16, COLS)
+            high = dot(rows, wbuf[512:1024, 0:COLS]).reshape(NY, 16, COLS)
             zs[2 * g : 2 * g + 2] = (low[:, :8] + high[:, 8:]).reshape(2, 32, COLS).astype(BF16)
         zr[z] = zs[z]
         for k in range(1, NZ):
@@ -244,37 +305,50 @@
         wait(h2r.at[pl.ds(0, NX - 1)], d_recv.at[4])
         hand_ref[...] = dot(regroup_last(), h2r[...].reshape(128, 128)).astype(BF16)
 
-    def slot(s, carry):
-        @pl.when((s >= 4) & (s < ITEMS))
+    send_context()
+    gather(0)
+    pass_weights(0)
+    gather(1)
+    pass_weights(1)
+    project(0, 3, (0,))
+    take_weights(0)
+    take_weights(1)
+    project(0, 3, (1, 2))
+    stage(0, 0)
+    stage(1, 0)
+    pass_context()
+    gather(2)
+    pass_last_weights()
+    project(3, 1, (0, 1, 2))
+    take_weights(2)
+    project(0, 4, (3,))
+    starts = [(0, 1), (2, 3), (4,), (5,), (6, 7)]
+    before = {
+        2: lambda: (gather(3), project(4, 1, range(NX))),
+        3: lambda: (gather(4), project(5, 1, range(NX)), project_decode()),
+        4: lambda: (gather(5), project(6, 1, range(NX)), gather(6), project(7, 1, range(NX))),
+        5: hand_over,
+        6: hand_on,
+        7: take,
+    }
+    for slot in range(1, 9):
+        if slot in before:
+            before[slot]()
+        for t in range(5):
+            for r in starts[slot - t] if 0 <= slot - t < len(starts) else ():
+                stage(r, t) if t < 4 else finish(r)
+
+    wait(rec_ref, out_recv.at[0])
+    for r in range(ROUNDS):
+        @pl.when(jnp.logical_not(place(r)[3]))
         def _():
-            gather(s - 1)
-
-        @pl.when(s < ITEMS)
-        def _():
-            rows = abuf[s]
-            for j in range(NX):
-                pbuf[s, j] = dot(rows, w_ref[...] if j == 0 else wbuf[j - 1])
-
-        for way in (0, 1):
-            for root in (0, 1):
-                chain(s, way, root)
-        for step, task in ((3, project_decode), (5, hand_over), (7, hand_on), (9, take)):
-            pl.when(s == step)(task)
-        return carry
-
-    lax.fori_loop(0, SLOTS, slot, 0)
-
-    @pl.when(x != z // 2)
-    def _():
-        wait(rec_ref, out_recv.at[0])
-
-    for way in (0, 1):
-        wait(sbuf.at[way], c_send.at[way])
-        wait(abuf.at[pl.ds(0, 7), pl.ds(0, HALF)], a_send.at[way])
-    wait(wbuf.at[pl.ds(0, 2), mine], w_send.at[0])
-    for k in (0, 1):
-        wait(wbuf.at[k, quarter[k]], w_send.at[0])
-    wait(wbuf.at[:, mine], w_send.at[1])
+            wait(sbuf.at[r, 7], f_send.at[r])
+
+    wait(sbuf.at[:, pl.ds(0, 7)], c_send.at[0])
+    for h in (0, 1):
+        wait(abuf.at[pl.ds(0, 7), pl.ds(0, HALF)], a_send.at[h])
+    wait(wbuf.at[pl.ds(0, 512), pl.ds(0, 3 * COLS)], w_send.at[0])
+    wait(wbuf.at[pl.ds(0, 512), pl.ds(0, 3 * COLS)], w_send.at[1])
     wait(cbuf.at[0, pl.ds(0, NY - 1)], d_send.at[0])
     wait(cbuf.at[pl.ds(0, NX - 1)], d_send.at[1])
     wait(zs.at[pl.ds(0, NZ - 1)], d_send.at[2])
@@ -292,14 +366,19 @@
             jax.ShapeDtypeStruct((128, 128), BF16),
             jax.ShapeDtypeStruct((512, COLS), BF16),
         ),
-        in_specs=[vmem, vmem, vmem, pl.BlockSpec(memory_space=pltpu.SMEM), vmem, vmem, vmem],
+        in_specs=[pl.BlockSpec(memory_space=pltpu.HBM)] * 7,
         out_specs=(vmem, vmem, vmem),
         scratch_shapes=[
+            pltpu.VMEM((8, WIDTH), BF16),
+            pltpu.VMEM((16, HEAD_SIZE), BF16),
+            pltpu.VMEM((8, 2 * CACHED_POSITIONS, HEAD_SIZE), BF16),
+            pltpu.SMEM((8,), jnp.int32),
+            pltpu.VMEM((1, 32), jnp.int32),
             pltpu.VMEM((ITEMS, BLOCK, WIDTH), BF16),
-            pltpu.VMEM((NX - 1, WIDTH, COLS), BF16),
-            pltpu.VMEM((ITEMS, NX, BLOCK, COLS), F32),
-            pltpu.VMEM((2, ITEMS, NX, HALF, COLS), BF16),
-            pltpu.VMEM((2, ITEMS, NX, HALF, COLS), BF16),
+            pltpu.VMEM((WIDTH, NX * COLS), BF16),
+            pltpu.VMEM((ROUNDS * NZ, HALF, COLS), F32),
+            pltpu.VMEM((ROUNDS, NZ - 1, HALF, COLS), BF16),
+            pltpu.VMEM((ROUNDS, NZ, HALF, COLS), BF16),
             pltpu.VMEM((NX, NY, 16, 512), BF16),
             pltpu.VMEM((NZ, 32, COLS), BF16),
             pltpu.VMEM((NZ, 32, COLS), BF16),
@@ -307,18 +386,20 @@
             pltpu.VMEM((NY, 16, 128), BF16),
             pltpu.VMEM((NX, 32, 128), BF16),
             pltpu.VMEM((NX, 32, 128), BF16),
+            dma((7,)),
             dma((2,)),
             dma((2, 7)),
             dma((2,)),
-            dma((7,)),
+            dma((6, 2)),
             dma((5,)),
             dma((5,)),
-            dma((2,)),
-            dma((2, ITEMS, NX)),
+            dma((1,)),
+            dma((ROUNDS, NZ - 1)),
+            dma((ROUNDS,)),
             dma((1,)),
         ],
         compiler_params=pltpu.CompilerParams(
-            collective_id=0, has_side_effects=True, vmem_limit_bytes=48 * 1024 * 1024
+            collective_id=0, has_side_effects=True, vmem_limit_bytes=63 * 1024 * 1024
         ),
         cost_estimate=pl.CostEstimate(flops=2300000000, bytes_accessed=2500000, transcendentals=33000),
         name="project",

time: 96.6 us -> 80.1 us (0.83)
  the two profiles are of different devices: /device:TPU:6 before, /device:TPU:60 now
where the time goes in v2:
time: 80.1 us; the launch traced here: 79.9 us
  Pallas kernels  75.6 us (94%)
  local copies, waits for them, and re-layouts  3.67 us (5%)
    pallas_call x1, Pallas kernels, local(): pl.pallas_call(kernel, out_shape=(jax.ShapeDtypeStruct((32, COLS), BF16),...  75.6 us
    unnamed x4, local copies, waits for them, and re-layouts  2.28 us

profile of v2, /device:TPU:60, one launch (start us, length us, event | category | flops | bytes accessed | tf_op | source)
XLA Modules:
  0.0 79.9 jit_solution(11978252122033003923)
XLA Ops:
  0.6 75.6 %project.1 = (bf16[32,256]{1,0:T(8,128)(2,1)}, bf16[128,128]{1,0:T(8,128)(2,1)}, bf16[512,256]{1,0:T(8,128)(2,1)}) custom-call(bf16[8,1024]{1,0:T(8,128)(2,1)} %q_hbm.1, bf16[16,128]{1,0:T(8,128)(2,1)} %bitcast.4, bf16[8,512,128]{2,1,0:T(8,128)(2,1)} %bitcast.3, s32[8]{0:T(128)} %len_hbm.1, s32[1,32]{1,0:T(1,128)} %bitcast.5, bf16[1024,256]{1,0:T(8,128)(2,1)} %w_hbm.1, ...), custom_call_target="tpu_custom_call" | custom-call | flops 2300000000 | bytes 2500000 | tf_op jit(solution)/shard_map/project/pallas_call | solution.py:362
  76.2 0.0 copy-start
  76.2 1.4 %reshape.21 = bf16[1,1,1,2,8192]{4,3,2,1,0:T(2,128)(2,1)} reshape(bf16[128,128]{1,0:T(8,128)(2,1)} %get-tuple-element.7) | data formatting | bytes 65536 | tf_op jit(solution)/shard_map/reshape | solution.py:415
  77.6 0.0 copy-done
  77.6 0.6 copy.12
  78.2 1.7 %copy.13 = bf16[512,256]{1,0:T(8,128)(2,1)} copy(bf16[512,256]{1,0:T(8,128)(2,1)} %get-tuple-element.14) | data formatting | bytes 524288
Async XLA Ops:
  76.2 1.4 %copy-start = (bf16[32,256]{1,0:T(8,128)(2,1)S(1)}, bf16[32,256]{1,0:T(8,128)(2,1)}, u32[]{:S(2)}) copy-start(bf16[32,256]{1,0:T(8,128)(2,1)} %get-tuple-element.12) | copy-start | bytes 49156

commit v3 on v2

--- a/solution.py
+++ b/solution.py
@@ -1,3 +1,5 @@
+import functools
+
 import jax
 import jax.numpy as jnp
 from jax import lax
@@ -16,7 +18,7 @@
 ITEMS = NY
 CHUNKS = [(0, 0), (1, 0), (2, 0), (0, 1), (0, 2), (1, 1), (1, 2), (2, 1), (2, 2), (3, 0), (3, 1), (3, 2)]
 CHUNKS += [(m, 3) for m in range(4)] + [(m, j) for m in range(4, ITEMS) for j in range(NX)]
-ROUNDS = 8
+ROUNDS, LATE = 8, 6
 MESH_ID = pl.DeviceIdType.MESH
 BF16, F32 = jnp.bfloat16, jnp.float32
 
@@ -100,8 +102,8 @@
     q_hbm, f_hbm, c_hbm, len_hbm, dest_hbm, w_hbm, a_hbm,
     dec_ref, hand_ref, rec_ref,
     q_ref, f_ref, c_ref, len_ref, dest_ref,
-    abuf, wbuf, pbuf, rbuf, sbuf, cbuf, zs, zr, h1s, h1r, h2s, h2r,
-    in_sem, a_send, a_recv, w_send, w_recv, d_send, d_recv, c_send, c_recv, f_send, out_recv,
+    abuf, wbuf, pbuf, rbuf, sbuf, moved, xs, xr, ls, lr, cbuf, zs, zr, h1s, h1r, h2s, h2r,
+    in_sem, a_send, a_recv, w_send, w_recv, d_send, d_recv, c_send, c_recv, m_send, m_recv, f_send, x_send, x_recv, l_send, l_recv, out_recv,
 ):
     core, seq, z = lax.axis_index("dp"), lax.axis_index("seq"), lax.axis_index("tensor")
     x, y = seq // NY, seq % NY
@@ -231,16 +233,19 @@
             out = jnp.where(own_chunk == k, values[k], out)
         return out
 
-    def place(r):
-        chunks = CHUNKS[4 * r : 4 * r + 4]
-        j = pick([c[1] for c in chunks])
-        dx = jnp.where(j == 1, NX - 1, jnp.where(j == 0, 0, j - 1))
-        steps = pick([(c[0] + 1) // 2 for c in chunks])
-        sign = pick([1 if c[0] % 2 == 0 else -1 for c in chunks]) * (1 - 2 * own_half)
-        item_y = lax.rem(y + sign * steps + 2 * NY, NY)
-        dz = 2 * x + item_y // 4 - z
-        row = pl.multiple_of(lax.rem(item_y, 4) * BLOCK + own_half * HALF, HALF)
-        return dx, dz, row, (dx == 0) & (dz == 0)
+    def spot(m, h):
+        steps = (m + 1) // 2
+        sign = jnp.where(lax.rem(m + h, 2) == 0, 1, -1)
+        return lax.rem(y + sign * steps + 2 * NY, NY)
+
+    def shift(j):
+        return jnp.where(j == 1, NX - 1, jnp.where(j == 0, 0, j - 1))
+
+    def out_rows(item_y, h):
+        return rec_ref.at[pl.ds(pl.multiple_of(lax.rem(item_y, 4) * BLOCK + h * HALF, HALF), HALF)]
+
+    def keep(src, rows):
+        pltpu.make_async_copy(src, rows, out_recv.at[0]).start()
 
     def finish(r):
         total = piece(r, 0)
@@ -248,16 +253,89 @@
             wait(rbuf.at[r, slot], c_recv.at[r, slot])
             total = total + rbuf[r, slot].astype(F32)
         sbuf[r, 7] = total.astype(BF16)
-        dx, dz, row, stays = place(r)
-        rows = rec_ref.at[pl.ds(row, HALF)]
-
-        @pl.when(stays)
+        j = pick([c[1] for c in CHUNKS[4 * r : 4 * r + 4]])
+
+        @pl.when(j == 0)
         def _():
-            pltpu.make_async_copy(sbuf.at[r, 7], rows, out_recv.at[0]).start()
-
-        @pl.when(jnp.logical_not(stays))
+            pltpu.make_async_copy(sbuf.at[r, 7], moved.at[r], m_recv.at[r]).start()
+
+        @pl.when(j > 0)
         def _():
-            send(sbuf.at[r, 7], rows, f_send.at[r], out_recv.at[0], at(dx=dx, dz=dz))
+            send(sbuf.at[r, 7], moved.at[r], m_send.at[r], m_recv.at[r], at(dx=shift(j)))
+
+    def home(r):
+        chunks = CHUNKS[4 * r : 4 * r + 4]
+        item_y = spot(pick([c[0] for c in chunks]), own_half)
+        from_x = lax.rem(x - shift(pick([c[1] for c in chunks])) + NX, NX)
+        return out_rows(item_y, own_half), 2 * from_x + item_y // 4
+
+    def deliver(r):
+        wait(moved.at[r], m_recv.at[r])
+        rows, to_z = home(r)
+
+        @pl.when(to_z == z)
+        def _():
+            keep(moved.at[r], rows)
+
+        @pl.when(to_z != z)
+        def _():
+            send(moved.at[r], rows, f_send.at[r], out_recv.at[0], at(dz=to_z - z))
+
+    def exchange(r):
+        e = r - LATE
+        for j in range(NX):
+            for h in (0, 1):
+                part_sum = pbuf[8 * r + 2 * j + h].astype(BF16)
+                if j == 0:
+                    xr[e, 0, h] = part_sum
+                else:
+                    xs[e, j - 1, h] = part_sum
+            if j > 0:
+                send(xs.at[e, j - 1], xr.at[e, j], x_send.at[e, j - 1], x_recv.at[e, j - 1], at(dx=(0, 3, 1, 2)[j]))
+
+    def exchanged(r):
+        for j in range(1, NX):
+            wait(xr.at[r - LATE, j], x_recv.at[r - LATE, j - 1])
+
+    def late_messages(r, t, act):
+        for side in (0, 1):
+            if side > t:
+                continue
+            way = up if side == 0 else -up
+            slot = 4 * side + t - side
+            q = lax.rem(z + way * (4 - t) + NZ, NZ)
+            for h in (0, 1):
+                pl.when(spot(r, h) // 4 == lax.rem(q, 2))(functools.partial(act, r - LATE, t > side, way, slot, q, h))
+
+    def late_piece(e, q, h):
+        away = lax.rem(x - q // 2 + NX, NX)
+        j = jnp.where(away == 0, 0, jnp.where(away == 3, 1, away + 1))
+        return xr[e, j, h].astype(F32)
+
+    def late_send(e, later, way, slot, q, h):
+        total = late_piece(e, q, h)
+        if later:
+            wait(lr.at[e, slot - 1, h], l_recv.at[e, slot - 1, h])
+            total = total + lr[e, slot - 1, h].astype(F32)
+        ls[e, slot, h] = total.astype(BF16)
+        send(ls.at[e, slot, h], lr.at[e, slot, h], l_send.at[e, slot, h], l_recv.at[e, slot, h], at(dz=way))
+
+    def late_drain(e, later, way, slot, q, h):
+        wait(ls.at[e, slot, h], l_send.at[e, slot, h])
+
+    def late_finish(r):
+        e = r - LATE
+        for h in (0, 1):
+            item_y = spot(r, h)
+
+            @pl.when(item_y // 4 == lax.rem(z, 2))
+            def _():
+                total = late_piece(e, z, h)
+                for slot in (3, 6):
+                    wait(lr.at[e, slot, h], l_recv.at[e, slot, h])
+                    total = total + lr[e, slot, h].astype(F32)
+                ls[e, 7, h] = total.astype(BF16)
+                keep(ls.at[e, 7, h], out_rows(item_y, h))
 
     def send_context():
         cbuf[x, y] = attend(q_ref, f_ref, c_ref, len_ref)
@@ -322,28 +400,66 @@
     project(3, 1, (0, 1, 2))
     take_weights(2)
     project(0, 4, (3,))
-    starts = [(0, 1), (2, 3), (4,), (5,), (6, 7)]
-    before = {
-        2: lambda: (gather(3), project(4, 1, range(NX))),
-        3: lambda: (gather(4), project(5, 1, range(NX)), project_decode()),
-        4: lambda: (gather(5), project(6, 1, range(NX)), gather(6), project(7, 1, range(NX))),
-        5: hand_over,
-        6: hand_on,
-        7: take,
-    }
-    for slot in range(1, 9):
-        if slot in before:
-            before[slot]()
-        for t in range(5):
-            for r in starts[slot - t] if 0 <= slot - t < len(starts) else ():
-                stage(r, t) if t < 4 else finish(r)
+    starts = [(0, 1), (2, 3), (4,), (5,)]
+
+    def slot(number):
+        for t in range(6):
+            for r in starts[number - t] if 0 <= number - t < len(starts) else ():
+                stage(r, t) if t < 4 else finish(r) if t == 4 else deliver(r)
+
+    def late(r, t):
+        if t == 0:
+            exchanged(r)
+        late_messages(r, t, late_send) if t < 4 else late_finish(r)
+
+    slot(1)
+    gather(3)
+    project(4, 1, range(NX))
+    slot(2)
+    gather(4)
+    project(5, 1, range(NX))
+    project_decode()
+    slot(3)
+    gather(5)
+    project(6, 1, range(NX))
+    exchange(6)
+    gather(6)
+    project(7, 1, range(NX))
+    exchange(7)
+    slot(4)
+    late(6, 0)
+    hand_over()
+    late(7, 0)
+    late(6, 1)
+    slot(5)
+    late(7, 1)
+    late(6, 2)
+    slot(6)
+    hand_on()
+    late(7, 2)
+    late(6, 3)
+    slot(7)
+    take()
+    late(7, 3)
+    late(6, 4)
+    slot(8)
+    late(7, 4)
 
     wait(rec_ref, out_recv.at[0])
-    for r in range(ROUNDS):
-        @pl.when(jnp.logical_not(place(r)[3]))
+    for r in range(LATE):
+        @pl.when(pick([c[1] for c in CHUNKS[4 * r : 4 * r + 4]]) > 0)
         def _():
-            wait(sbuf.at[r, 7], f_send.at[r])
-
+            wait(sbuf.at[r, 7], m_send.at[r])
+
+        @pl.when(home(r)[1] != z)
+        def _():
+            wait(moved.at[r], f_send.at[r])
+
+    for r in range(LATE, ROUNDS):
+        for t in range(4):
+            late_messages(r, t, late_drain)
+        for j in range(NX - 1):
+            wait(xs.at[r - LATE, j], x_send.at[r - LATE, j])
     wait(sbuf.at[:, pl.ds(0, 7)], c_send.at[0])
     for h in (0, 1):
         wait(abuf.at[pl.ds(0, 7), pl.ds(0, HALF)], a_send.at[h])
@@ -377,8 +493,13 @@
             pltpu.VMEM((ITEMS, BLOCK, WIDTH), BF16),
             pltpu.VMEM((WIDTH, NX * COLS), BF16),
             pltpu.VMEM((ROUNDS * NZ, HALF, COLS), F32),
-            pltpu.VMEM((ROUNDS, NZ - 1, HALF, COLS), BF16),
-            pltpu.VMEM((ROUNDS, NZ, HALF, COLS), BF16),
+            pltpu.VMEM((LATE, NZ - 1, HALF, COLS), BF16),
+            pltpu.VMEM((LATE, NZ, HALF, COLS), BF16),
+            pltpu.VMEM((LATE, HALF, COLS), BF16),
+            pltpu.VMEM((ROUNDS - LATE, NX - 1, 2, HALF, COLS), BF16),
+            pltpu.VMEM((ROUNDS - LATE, NX, 2, HALF, COLS), BF16),
+            pltpu.VMEM((ROUNDS - LATE, NZ, 2, HALF, COLS), BF16),
+            pltpu.VMEM((ROUNDS - LATE, NZ - 1, 2, HALF, COLS), BF16),
             pltpu.VMEM((NX, NY, 16, 512), BF16),
             pltpu.VMEM((NZ, 32, COLS), BF16),
             pltpu.VMEM((NZ, 32, COLS), BF16),
@@ -394,8 +515,14 @@
             dma((5,)),
             dma((5,)),
             dma((1,)),
-            dma((ROUNDS, NZ - 1)),
-            dma((ROUNDS,)),
+            dma((LATE, NZ - 1)),
+            dma((LATE,)),
+            dma((LATE,)),
+            dma((LATE,)),
+            dma((ROUNDS - LATE, NX - 1)),
+            dma((ROUNDS - LATE, NX - 1)),
+            dma((ROUNDS - LATE, NZ - 1, 2)),
+            dma((ROUNDS - LATE, NZ - 1, 2)),
             dma((1,)),
         ],
         compiler_params=pltpu.CompilerParams(

time: 80.1 us -> 71.7 us (0.90)
  the two profiles are of different devices: /device:TPU:60 before, /device:TPU:6 now
where the time goes in v3:
time: 71.7 us; the launch traced here: 70.6 us
  Pallas kernels  66.2 us (92%)
  local copies, waits for them, and re-layouts  3.67 us (5%)
    pallas_call x1, Pallas kernels, local(): pl.pallas_call(kernel, out_shape=(jax.ShapeDtypeStruct((32, COLS), BF16),...  66.2 us
    unnamed x4, local copies, waits for them, and re-layouts  2.28 us

profile of v3, /device:TPU:6, one launch (start us, length us, event | category | flops | bytes accessed | tf_op | source)
XLA Modules:
  0.0 70.6 jit_solution(18429943959104433245)
XLA Ops:
  0.6 66.2 %project.1 = (bf16[32,256]{1,0:T(8,128)(2,1)}, bf16[128,128]{1,0:T(8,128)(2,1)}, bf16[512,256]{1,0:T(8,128)(2,1)}) custom-call(bf16[8,1024]{1,0:T(8,128)(2,1)} %q_hbm.1, bf16[16,128]{1,0:T(8,128)(2,1)} %bitcast.4, bf16[8,512,128]{2,1,0:T(8,128)(2,1)} %bitcast.3, s32[8]{0:T(128)} %len_hbm.1, s32[1,32]{1,0:T(1,128)} %bitcast.5, bf16[1024,256]{1,0:T(8,128)(2,1)} %w_hbm.1, ...), custom_call_target="tpu_custom_call" | custom-call | flops 2300000000 | bytes 2500000 | tf_op jit(solution)/shard_map/project/pallas_call | solution.py:478
  66.9 0.0 copy-start
  66.9 1.4 %reshape.21 = bf16[1,1,1,2,8192]{4,3,2,1,0:T(2,128)(2,1)} reshape(bf16[128,128]{1,0:T(8,128)(2,1)} %get-tuple-element.7) | data formatting | bytes 65536 | tf_op jit(solution)/shard_map/reshape | solution.py:542
  68.3 0.0 copy-done
  68.3 0.6 copy.12
  68.9 1.7 %copy.13 = bf16[512,256]{1,0:T(8,128)(2,1)} copy(bf16[512,256]{1,0:T(8,128)(2,1)} %get-tuple-element.14) | data formatting | bytes 524288
Async XLA Ops:
  66.9 1.4 %copy-start = (bf16[32,256]{1,0:T(8,128)(2,1)S(1)}, bf16[32,256]{1,0:T(8,128)(2,1)}, u32[]{:S(2)}) copy-start(bf16[32,256]{1,0:T(8,128)(2,1)} %get-tuple-element.12) | copy-start | bytes 49156

commit v4 on v3

--- a/solution.py
+++ b/solution.py
@@ -18,7 +18,23 @@
 ITEMS = NY
 CHUNKS = [(0, 0), (1, 0), (2, 0), (0, 1), (0, 2), (1, 1), (1, 2), (2, 1), (2, 2), (3, 0), (3, 1), (3, 2)]
 CHUNKS += [(m, 3) for m in range(4)] + [(m, j) for m in range(4, ITEMS) for j in range(NX)]
-ROUNDS, LATE = 8, 6
+ROUNDS, LATE = 8, 4
+SHORT_HOPS = [
+    (0, 0, 4, 1, None), (0, 1, 3, 1, None), (1, 0, 3, 1, 0), (1, 1, 2, 1, 1), (2, 0, 2, 1, 2), (2, 1, 1, 1, 3),
+    (3, 0, 1, 1, 4),
+]
+HOPS = {r: SHORT_HOPS for r in range(LATE, ROUNDS)}
+
+ORDER = [
+    ("ctx",), ("g", 0), ("pw", 0), ("g", 1), ("pw", 1), ("pA",), ("tw", 0), ("tw", 1), ("pB",), ("s", 0, 0),
+    ("s", 1, 0), ("pctx",), ("g", 2), ("plw",), ("pC",), ("tw", 2), ("pD",), ("s", 2, 0), ("s", 3, 0), ("s", 0, 1),
+    ("s", 1, 1), ("g", 3), ("p", 4), ("x", 4), ("s", 2, 1), ("s", 3, 1), ("s", 0, 2), ("s", 1, 2), ("g", 4), ("p", 5),
+    ("x", 5), ("e", 4), ("l", 4, 0), ("pd",), ("s", 2, 2), ("s", 3, 2), ("s", 0, 3), ("s", 1, 3), ("g", 5), ("p", 6),
+    ("x", 6), ("e", 5), ("l", 5, 0), ("l", 4, 1), ("g", 6), ("p", 7), ("x", 7), ("s", 2, 3), ("s", 3, 3), ("e", 6),
+    ("l", 6, 0), ("f", 0), ("f", 1), ("l", 5, 1), ("l", 4, 2), ("e", 7), ("l", 7, 0), ("l", 6, 1), ("ho",), ("f", 2),
+    ("f", 3), ("d", 0), ("d", 1), ("l", 5, 2), ("l", 4, 3), ("l", 7, 1), ("l", 6, 2), ("l", 5, 3), ("hon",), ("F", 4),
+    ("l", 7, 2), ("l", 6, 3), ("d", 2), ("d", 3), ("F", 5), ("l", 7, 3), ("F", 6), ("take",), ("F", 7),
+]
 MESH_ID = pl.DeviceIdType.MESH
 BF16, F32 = jnp.bfloat16, jnp.float32
 
@@ -95,7 +111,7 @@
 
 def regroup_last():
     r, c = iota((128, 128), 0), iota((128, 128), 1)
-    return one_hot((r // 2 % 32) * 4 + (r // 64) * 2 + r % 2 == c)
+    return one_hot((r // 4) * 4 + (r % 2) * 2 + r // 2 % 2 == c)
 
 
 def kernel(
@@ -298,42 +314,43 @@
             wait(xr.at[r - LATE, j], x_recv.at[r - LATE, j - 1])
 
     def late_messages(r, t, act):
-        for side in (0, 1):
-            if side > t:
-                continue
-            way = up if side == 0 else -up
-            slot = 4 * side + t - side
-            q = lax.rem(z + way * (4 - t) + NZ, NZ)
-            for h in (0, 1):
-                pl.when(spot(r, h) // 4 == lax.rem(q, 2))(functools.partial(act, r - LATE, t > side, way, slot, q, h))
+        for k, (turn, side, far, hop, after) in enumerate(HOPS[r]):
+            if turn == t:
+                way = up if side == 0 else -up
+                q = lax.rem(z + way * far + NZ, NZ)
+                for h in (0, 1):
+                    pl.when(spot(r, h) // 4 == lax.rem(q, 2))(
+                        functools.partial(act, r - LATE, k, after, way * hop, q, h)
+                    )
 
     def late_piece(e, q, h):
         away = lax.rem(x - q // 2 + NX, NX)
         j = jnp.where(away == 0, 0, jnp.where(away == 3, 1, away + 1))
         return xr[e, j, h].astype(F32)
 
-    def late_send(e, later, way, slot, q, h):
+    def late_send(e, k, after, dz, q, h):
         total = late_piece(e, q, h)
-        if later:
-            wait(lr.at[e, slot - 1, h], l_recv.at[e, slot - 1, h])
-            total = total + lr[e, slot - 1, h].astype(F32)
-        ls[e, slot, h] = total.astype(BF16)
-        send(ls.at[e, slot, h], lr.at[e, slot, h], l_send.at[e, slot, h], l_recv.at[e, slot, h], at(dz=way))
-
-    def late_drain(e, later, way, slot, q, h):
-        wait(ls.at[e, slot, h], l_send.at[e, slot, h])
+        if after is not None:
+            wait(lr.at[e, after, h], l_recv.at[e, after, h])
+            total = total + lr[e, after, h].astype(F32)
+        ls[e, k, h] = total.astype(BF16)
+        send(ls.at[e, k, h], lr.at[e, k, h], l_send.at[e, k, h], l_recv.at[e, k, h], at(dz=dz))
+
+    def late_drain(e, k, after, dz, q, h):
+        wait(ls.at[e, k, h], l_send.at[e, k, h])
 
     def late_finish(r):
         e = r - LATE
+        ends = [k for k in range(NZ - 1) if k not in [hop[4] for hop in HOPS[r]]]
         for h in (0, 1):
             item_y = spot(r, h)
 
             @pl.when(item_y // 4 == lax.rem(z, 2))
             def _():
                 total = late_piece(e, z, h)
-                for slot in (3, 6):
-                    wait(lr.at[e, slot, h], l_recv.at[e, slot, h])
-                    total = total + lr[e, slot, h].astype(F32)
+                for k in ends:
+                    wait(lr.at[e, k, h], l_recv.at[e, k, h])
+                    total = total + lr[e, k, h].astype(F32)
                 ls[e, 7, h] = total.astype(BF16)
                 keep(ls.at[e, 7, h], out_rows(item_y, h))
 
@@ -381,69 +398,19 @@
 
     def take():
         wait(h2r.at[pl.ds(0, NX - 1)], d_recv.at[4])
-        hand_ref[...] = dot(regroup_last(), h2r[...].reshape(128, 128)).astype(BF16)
-
-    send_context()
-    gather(0)
-    pass_weights(0)
-    gather(1)
-    pass_weights(1)
-    project(0, 3, (0,))
-    take_weights(0)
-    take_weights(1)
-    project(0, 3, (1, 2))
-    stage(0, 0)
-    stage(1, 0)
-    pass_context()
-    gather(2)
-    pass_last_weights()
-    project(3, 1, (0, 1, 2))
-    take_weights(2)
-    project(0, 4, (3,))
-    starts = [(0, 1), (2, 3), (4,), (5,)]
-
-    def slot(number):
-        for t in range(6):
-            for r in starts[number - t] if 0 <= number - t < len(starts) else ():
-                stage(r, t) if t < 4 else finish(r) if t == 4 else deliver(r)
-
-    def late(r, t):
-        if t == 0:
-            exchanged(r)
-        late_messages(r, t, late_send) if t < 4 else late_finish(r)
-
-    slot(1)
-    gather(3)
-    project(4, 1, range(NX))
-    slot(2)
-    gather(4)
-    project(5, 1, range(NX))
-    project_decode()
-    slot(3)
-    gather(5)
-    project(6, 1, range(NX))
-    exchange(6)
-    gather(6)
-    project(7, 1, range(NX))
-    exchange(7)
-    slot(4)
-    late(6, 0)
-    hand_over()
-    late(7, 0)
-    late(6, 1)
-    slot(5)
-    late(7, 1)
-    late(6, 2)
-    slot(6)
-    hand_on()
-    late(7, 2)
-    late(6, 3)
-    slot(7)
-    take()
-    late(7, 3)
-    late(6, 4)
-    slot(8)
-    late(7, 4)
+        out = dot(regroup_last(), h2r[...].reshape(128, 128))
+        hand_ref[0, 0, 0] = jnp.concatenate([out[2 * k : 2 * k + 2] for k in range(64)], axis=1).astype(BF16)
+
+    tasks = {
+        "ctx": send_context, "pctx": pass_context, "pd": project_decode, "ho": hand_over, "hon": hand_on, "take": take,
+        "g": gather, "pw": pass_weights, "plw": pass_last_weights, "tw": take_weights,
+        "pA": lambda: project(0, 3, (0,)), "pB": lambda: project(0, 3, (1, 2)), "pC": lambda: project(3, 1, (0, 1, 2)),
+        "pD": lambda: project(0, 4, (3,)), "p": lambda m: project(m, 1, range(NX)),
+        "x": exchange, "e": exchanged, "s": stage, "f": finish, "d": deliver,
+        "l": lambda r, t: late_messages(r, t, late_send), "F": late_finish,
+    }
+    for name, *numbers in ORDER:
+        tasks[name](*numbers)
 
     wait(rec_ref, out_recv.at[0])
     for r in range(LATE):
@@ -472,14 +439,27 @@
     wait(h2s.at[pl.ds(0, NX - 1)], d_send.at[4])
 
 
+def emit(*refs):
+    given, out, held, sems = refs[:3], refs[3:6], refs[6:9], refs[9]
+    loads = [pltpu.make_async_copy(given[k], held[k], sems.at[0, k]) for k in range(3)]
+    stores = [pltpu.make_async_copy(held[k], out[k], sems.at[1, k]) for k in range(3)]
+    for load in loads:
+        load.start()
+    for load, store in zip(loads, stores):
+        load.wait()
+        store.start()
+    for store in stores:
+        store.wait()
+
+
 def local(query, fresh_key_value, cache, lengths, destination, out_weight, learner_ctx):
     vmem = pl.BlockSpec(memory_space=pltpu.VMEM)
     dma = pltpu.SemaphoreType.DMA
-    decoded, handed, recomputed = pl.pallas_call(
+    results = pl.pallas_call(
         kernel,
         out_shape=(
             jax.ShapeDtypeStruct((32, COLS), BF16),
-            jax.ShapeDtypeStruct((128, 128), BF16),
+            jax.ShapeDtypeStruct((1, 1, 1, 2, 8192), BF16),
             jax.ShapeDtypeStruct((512, COLS), BF16),
         ),
         in_specs=[pl.BlockSpec(memory_space=pltpu.HBM)] * 7,
@@ -539,7 +519,16 @@
         out_weight,
         learner_ctx,
     )
-    return decoded, handed.reshape(1, 1, 1, 2, 8192), recomputed
+    in_hbm = pl.BlockSpec(memory_space=pltpu.HBM)
+    return pl.pallas_call(
+        emit,
+        out_shape=tuple(jax.ShapeDtypeStruct(r.shape, r.dtype) for r in results),
+        in_specs=[in_hbm] * 3,
+        out_specs=(in_hbm,) * 3,
+        scratch_shapes=[pltpu.VMEM(r.shape, r.dtype) for r in results] + [dma((2, 3))],
+        compiler_params=pltpu.CompilerParams(vmem_limit_bytes=63 * 1024 * 1024),
+        name="emit",
+    )(*results)
 
 
 def solution(mesh):

time: 71.7 us -> 67.6 us (0.943)
  the two profiles are of different devices: /device:TPU:6 before, /device:TPU:4 now
where the time goes in v4:
time: 67.6 us; the launch traced here: 67.4 us
  Pallas kernels  66.7 us (99%)
    pallas_call x1, Pallas kernels, local(): pl.pallas_call(kernel, out_shape=(jax.ShapeDtypeStruct((32, COLS), BF16),...  65 us
    pallas_call x1, Pallas kernels, local(): pl.pallas_call(emit, out_shape=tuple((jax.ShapeDtypeStruct(r.shape, r.dty...  1.74 us

profile of v4, /device:TPU:4, one launch (start us, length us, event | category | flops | bytes accessed | tf_op | source)
XLA Modules:
  0.0 67.4 jit_solution(11209960759295337907)
XLA Ops:
  0.6 65.0 %project.1 = (bf16[32,256]{1,0:T(8,128)(2,1)}, bf16[1,1,1,2,8192]{4,3,2,1,0:T(2,128)(2,1)}, bf16[512,256]{1,0:T(8,128)(2,1)}) custom-call(bf16[8,1024]{1,0:T(8,128)(2,1)} %q_hbm.1, bf16[16,128]{1,0:T(8,128)(2,1)} %bitcast.4, bf16[8,512,128]{2,1,0:T(8,128)(2,1)} %bitcast.3, s32[8]{0:T(128)} %len_hbm.1, s32[1,32]{1,0:T(1,128)} %bitcast.5, ...), custom_call_target="tpu_custom_call" | custom-call | flops 2300000000 | bytes 2500000 | tf_op jit(solution)/shard_map/project/pallas_call | solution.py:458
  65.6 1.7 %emit.1 = (bf16[32,256]{1,0:T(8,128)(2,1)}, bf16[1,1,1,2,8192]{4,3,2,1,0:T(2,128)(2,1)}, bf16[512,256]{1,0:T(8,128)(2,1)}) custom-call(bf16[32,256]{1,0:T(8,128)(2,1)} %get-tuple-element.6.refs_0_, bf16[1,1,1,2,8192]{4,3,2,1,0:T(2,128)(2,1)} %get-tuple-element.7.refs_1_, bf16[512,256]{1,0:T(8,128)(2,1)} %get-tuple-element.8.refs_2_), custom_call_target="tpu_custom_call" | custom-call | tf_op jit(solution)/shard_map/emit/pallas_call | solution.py:523

commit v5 on v4

--- a/solution.py
+++ b/solution.py
@@ -27,13 +27,13 @@
 
 ORDER = [
     ("ctx",), ("g", 0), ("pw", 0), ("g", 1), ("pw", 1), ("pA",), ("tw", 0), ("tw", 1), ("pB",), ("s", 0, 0),
-    ("s", 1, 0), ("pctx",), ("g", 2), ("plw",), ("pC",), ("tw", 2), ("pD",), ("s", 2, 0), ("s", 3, 0), ("s", 0, 1),
-    ("s", 1, 1), ("g", 3), ("p", 4), ("x", 4), ("s", 2, 1), ("s", 3, 1), ("s", 0, 2), ("s", 1, 2), ("g", 4), ("p", 5),
-    ("x", 5), ("e", 4), ("l", 4, 0), ("pd",), ("s", 2, 2), ("s", 3, 2), ("s", 0, 3), ("s", 1, 3), ("g", 5), ("p", 6),
-    ("x", 6), ("e", 5), ("l", 5, 0), ("l", 4, 1), ("g", 6), ("p", 7), ("x", 7), ("s", 2, 3), ("s", 3, 3), ("e", 6),
-    ("l", 6, 0), ("f", 0), ("f", 1), ("l", 5, 1), ("l", 4, 2), ("e", 7), ("l", 7, 0), ("l", 6, 1), ("ho",), ("f", 2),
-    ("f", 3), ("d", 0), ("d", 1), ("l", 5, 2), ("l", 4, 3), ("l", 7, 1), ("l", 6, 2), ("l", 5, 3), ("hon",), ("F", 4),
-    ("l", 7, 2), ("l", 6, 3), ("d", 2), ("d", 3), ("F", 5), ("l", 7, 3), ("F", 6), ("take",), ("F", 7),
+    ("s", 1, 0), ("g", 2), ("plw",), ("pC",), ("tw", 2), ("pD",), ("s", 2, 0), ("s", 3, 0), ("s", 0, 1), ("s", 1, 1),
+    ("g", 3), ("cs",), ("p", 4), ("x", 4), ("s", 2, 1), ("s", 3, 1), ("s", 0, 2), ("s", 1, 2), ("g", 4), ("p", 5),
+    ("x", 5), ("e", 4), ("l", 4, 0), ("s", 2, 2), ("s", 3, 2), ("s", 0, 3), ("s", 1, 3), ("g", 5), ("p", 6), ("x", 6),
+    ("e", 5), ("l", 5, 0), ("l", 4, 1), ("pd",), ("g", 6), ("p", 7), ("x", 7), ("s", 2, 3), ("s", 3, 3), ("e", 6),
+    ("l", 6, 0), ("sd",), ("f", 0), ("f", 1), ("l", 5, 1), ("l", 4, 2), ("e", 7), ("l", 7, 0), ("l", 6, 1), ("ho",),
+    ("f", 2), ("f", 3), ("d", 0), ("d", 1), ("l", 5, 2), ("l", 4, 3), ("l", 7, 1), ("l", 6, 2), ("l", 5, 3), ("hon",),
+    ("F", 4), ("l", 7, 2), ("l", 6, 3), ("d", 2), ("d", 3), ("F", 5), ("l", 7, 3), ("F", 6), ("take",), ("F", 7),
 ]
 MESH_ID = pl.DeviceIdType.MESH
 BF16, F32 = jnp.bfloat16, jnp.float32
@@ -118,7 +118,7 @@
     q_hbm, f_hbm, c_hbm, len_hbm, dest_hbm, w_hbm, a_hbm,
     dec_ref, hand_ref, rec_ref,
     q_ref, f_ref, c_ref, len_ref, dest_ref,
-    abuf, wbuf, pbuf, rbuf, sbuf, moved, xs, xr, ls, lr, cbuf, zs, zr, h1s, h1r, h2s, h2r,
+    abuf, wbuf, pbuf, rbuf, sbuf, moved, xs, xr, ls, lr, cbuf, xd, zs, zr, h1s, h1r, h2s, h2r,
     in_sem, a_send, a_recv, w_send, w_recv, d_send, d_recv, c_send, c_recv, m_send, m_recv, f_send, x_send, x_recv, l_send, l_recv, out_recv,
 ):
     core, seq, z = lax.axis_index("dp"), lax.axis_index("seq"), lax.axis_index("tensor")
@@ -354,23 +354,27 @@
                 ls[e, 7, h] = total.astype(BF16)
                 keep(ls.at[e, 7, h], out_rows(item_y, h))
 
+    def make_context():
+        cbuf[y] = attend(q_ref, f_ref, c_ref, len_ref)
+
     def send_context():
-        cbuf[x, y] = attend(q_ref, f_ref, c_ref, len_ref)
         for k in range(1, NY):
-            send(cbuf.at[x, y], cbuf.at[x, y], d_send.at[0], d_recv.at[0], at(dy=k))
-
-    def pass_context():
-        wait(cbuf.at[x, pl.ds(0, NY - 1)], d_recv.at[0])
-        for k in range(1, NX):
-            send(cbuf.at[x], cbuf.at[x], d_send.at[1], d_recv.at[1], at(dx=k))
+            send(cbuf.at[y], cbuf.at[y], d_send.at[0], d_recv.at[0], at(dy=k))
 
     def project_decode():
-        wait(cbuf.at[pl.ds(0, NX - 1)], d_recv.at[1])
-        for g in range(NX):
-            rows = cbuf[g].reshape(NY * 16, 512)
-            low = dot(rows, wbuf[0:512, 0:COLS]).reshape(NY, 16, COLS)
-            high = dot(rows, wbuf[512:1024, 0:COLS]).reshape(NY, 16, COLS)
-            zs[2 * g : 2 * g + 2] = (low[:, :8] + high[:, 8:]).reshape(2, 32, COLS).astype(BF16)
+        wait(cbuf.at[pl.ds(0, NY - 1)], d_recv.at[0])
+        rows = cbuf[...].reshape(NY * 16, 512)
+        low = dot(rows, wbuf[0:512]).reshape(NY, 16, NX * COLS)
+        high = dot(rows, wbuf[512:1024]).reshape(NY, 16, NX * COLS)
+        terms = (low[:, :8] + high[:, 8:]).reshape(2, 32, NX * COLS)
+        here = pl.ds(2 * x, 2)
+        zs[here] = terms[:, :, 0:COLS].astype(BF16)
+        for j in range(1, NX):
+            xd[j - 1] = terms[:, :, j * COLS : (j + 1) * COLS].astype(BF16)
+            send(xd.at[j - 1], zs.at[here], d_send.at[1], d_recv.at[1], at(dx=(0, 3, 1, 2)[j]))
+
+    def spread_decode():
+        wait(zs.at[pl.ds(0, 6)], d_recv.at[1])
         zr[z] = zs[z]
         for k in range(1, NZ):
             send(zs.at[lax.rem(z + k, NZ)], zr.at[z], d_send.at[2], d_recv.at[2], at(dz=k))
@@ -402,7 +406,7 @@
         hand_ref[0, 0, 0] = jnp.concatenate([out[2 * k : 2 * k + 2] for k in range(64)], axis=1).astype(BF16)
 
     tasks = {
-        "ctx": send_context, "pctx": pass_context, "pd": project_decode, "ho": hand_over, "hon": hand_on, "take": take,
+        "ctx": make_context, "cs": send_context, "pd": project_decode, "sd": spread_decode, "ho": hand_over, "hon": hand_on, "take": take,
         "g": gather, "pw": pass_weights, "plw": pass_last_weights, "tw": take_weights,
         "pA": lambda: project(0, 3, (0,)), "pB": lambda: project(0, 3, (1, 2)), "pC": lambda: project(3, 1, (0, 1, 2)),
         "pD": lambda: project(0, 4, (3,)), "p": lambda m: project(m, 1, range(NX)),
@@ -432,8 +436,8 @@
         wait(abuf.at[pl.ds(0, 7), pl.ds(0, HALF)], a_send.at[h])
     wait(wbuf.at[pl.ds(0, 512), pl.ds(0, 3 * COLS)], w_send.at[0])
     wait(wbuf.at[pl.ds(0, 512), pl.ds(0, 3 * COLS)], w_send.at[1])
-    wait(cbuf.at[0, pl.ds(0, NY - 1)], d_send.at[0])
-    wait(cbuf.at[pl.ds(0, NX - 1)], d_send.at[1])
+    wait(cbuf.at[pl.ds(0, NY - 1)], d_send.at[0])
+    wait(xd, d_send.at[1])
     wait(zs.at[pl.ds(0, NZ - 1)], d_send.at[2])
     wait(h1s.at[pl.ds(0, NY - 1)], d_send.at[3])
     wait(h2s.at[pl.ds(0, NX - 1)], d_send.at[4])
@@ -463,7 +467,7 @@
             jax.ShapeDtypeStruct((512, COLS), BF16),
         ),
         in_specs=[pl.BlockSpec(memory_space=pltpu.HBM)] * 7,
-        out_specs=(vmem, vmem, vmem),
+        out_specs=(vmem, vmem, pl.BlockSpec(memory_space=pltpu.HBM)),
         scratch_shapes=[
             pltpu.VMEM((8, WIDTH), BF16),
             pltpu.VMEM((16, HEAD_SIZE), BF16),
@@ -480,7 +484,8 @@
             pltpu.VMEM((ROUNDS - LATE, NX, 2, HALF, COLS), BF16),
             pltpu.VMEM((ROUNDS - LATE, NZ, 2, HALF, COLS), BF16),
             pltpu.VMEM((ROUNDS - LATE, NZ - 1, 2, HALF, COLS), BF16),
-            pltpu.VMEM((NX, NY, 16, 512), BF16),
+            pltpu.VMEM((NY, 16, 512), BF16),
+            pltpu.VMEM((NX - 1, 2, 32, COLS), BF16),
             pltpu.VMEM((NZ, 32, COLS), BF16),
             pltpu.VMEM((NZ, 32, COLS), BF16),
             pltpu.VMEM((NY, 16, 128), BF16),

time: 67.6 us -> 66.8 us (0.988)
  the two profiles are of different devices: /device:TPU:4 before, /device:TPU:12 now
where the time goes in v5:
time: 66.8 us; the launch traced here: 66.6 us
  Pallas kernels  66 us (99%)
    pallas_call x1, Pallas kernels, local(): pl.pallas_call(kernel, out_shape=(jax.ShapeDtypeStruct((32, COLS), BF16),...  64.2 us
    pallas_call x1, Pallas kernels, local(): pl.pallas_call(emit, out_shape=tuple((jax.ShapeDtypeStruct(r.shape, r.dty...  1.74 us

profile of v5, /device:TPU:12, one launch (start us, length us, event | category | flops | bytes accessed | tf_op | source)
XLA Modules:
  0.0 66.6 jit_solution(8179941638607884524)
XLA Ops:
  0.6 64.2 %project.1 = (bf16[32,256]{1,0:T(8,128)(2,1)}, bf16[1,1,1,2,8192]{4,3,2,1,0:T(2,128)(2,1)}, bf16[512,256]{1,0:T(8,128)(2,1)}) custom-call(bf16[8,1024]{1,0:T(8,128)(2,1)} %q_hbm.1, bf16[16,128]{1,0:T(8,128)(2,1)} %bitcast.4, bf16[8,512,128]{2,1,0:T(8,128)(2,1)} %bitcast.3, s32[8]{0:T(128)} %len_hbm.1, s32[1,32]{1,0:T(1,128)} %bitcast.5, ...), custom_call_target="tpu_custom_call" | custom-call | flops 2300000000 | bytes 2500000 | tf_op jit(solution)/shard_map/project/pallas_call | solution.py:462
  64.9 1.7 %emit.1 = (bf16[32,256]{1,0:T(8,128)(2,1)}, bf16[1,1,1,2,8192]{4,3,2,1,0:T(2,128)(2,1)}, bf16[512,256]{1,0:T(8,128)(2,1)}) custom-call(bf16[32,256]{1,0:T(8,128)(2,1)} %get-tuple-element.6.refs_0_, bf16[1,1,1,2,8192]{4,3,2,1,0:T(2,128)(2,1)} %get-tuple-element.7.refs_1_, bf16[512,256]{1,0:T(8,128)(2,1)} %get-tuple-element.8.refs_2_), custom_call_target="tpu_custom_call" | custom-call | tf_op jit(solution)/shard_map/emit/pallas_call | solution.py:528

commit v6 on v5

--- a/solution.py
+++ b/solution.py
@@ -155,7 +155,7 @@
     ]
     for load in loads:
         load.start()
-    for load in loads:
+    for load in loads[:2]:
         load.wait()
     pl.semaphore_wait(barrier, len(partners))
 
@@ -355,6 +355,8 @@
                 keep(ls.at[e, 7, h], out_rows(item_y, h))
 
     def make_context():
+        for load in loads[2:]:
+            load.wait()
         cbuf[y] = attend(q_ref, f_ref, c_ref, len_ref)
 
     def send_context():

time: 66.8 us -> 67.1 us (level)
  the two profiles are of different devices: /device:TPU:12 before, /device:TPU:72 now
where the time goes in v6:
time: 67.1 us; the launch traced here: 66.9 us
  Pallas kernels  66.2 us (99%)
    pallas_call x1, Pallas kernels, local(): pl.pallas_call(kernel, out_shape=(jax.ShapeDtypeStruct((32, COLS), BF16),...  64.5 us
    pallas_call x1, Pallas kernels, local(): pl.pallas_call(emit, out_shape=tuple((jax.ShapeDtypeStruct(r.shape, r.dty...  1.74 us

profile of v6, /device:TPU:72, one launch (start us, length us, event | category | flops | bytes accessed | tf_op | source)
XLA Modules:
  0.0 66.9 jit_solution(5882608613491884322)
XLA Ops:
  0.6 64.5 %project.1 = (bf16[32,256]{1,0:T(8,128)(2,1)}, bf16[1,1,1,2,8192]{4,3,2,1,0:T(2,128)(2,1)}, bf16[512,256]{1,0:T(8,128)(2,1)}) custom-call(bf16[8,1024]{1,0:T(8,128)(2,1)} %q_hbm.1, bf16[16,128]{1,0:T(8,128)(2,1)} %bitcast.4, bf16[8,512,128]{2,1,0:T(8,128)(2,1)} %bitcast.3, s32[8]{0:T(128)} %len_hbm.1, s32[1,32]{1,0:T(1,128)} %bitcast.5, ...), custom_call_target="tpu_custom_call" | custom-call | flops 2300000000 | bytes 2500000 | tf_op jit(solution)/shard_map/project/pallas_call | solution.py:464
  65.1 1.7 %emit.1 = (bf16[32,256]{1,0:T(8,128)(2,1)}, bf16[1,1,1,2,8192]{4,3,2,1,0:T(2,128)(2,1)}, bf16[512,256]{1,0:T(8,128)(2,1)}) custom-call(bf16[32,256]{1,0:T(8,128)(2,1)} %get-tuple-element.6.refs_0_, bf16[1,1,1,2,8192]{4,3,2,1,0:T(2,128)(2,1)} %get-tuple-element.7.refs_1_, bf16[512,256]{1,0:T(8,128)(2,1)} %get-tuple-element.8.refs_2_), custom_call_target="tpu_custom_call" | custom-call | tf_op jit(solution)/shard_map/emit/pallas_call | solution.py:530
